TPU v7x, 32 devices: a whole 2x2x4 slice. The times are simulated.
32 devices in a mesh: dp: 2 (over x), expert: 16 (over z, y, core).
Axes of the slice: x: 2, y: 2, z: 4, core: 2. Of those that a mesh axis runs over, the one named last changes fastest.
Arguments:
- tokens: bfloat16 [32, 576, 768], P(('dp', 'expert')), may hold values from -6 to 6
- cotangent: bfloat16 [32, 576, 768], P(('dp', 'expert')), may hold values from -6 to 6
- expert_choice: int32 [32, 576, 2], P(('dp', 'expert')), may hold values from 0 to 15, all different within a row
- priority: int32 [32, 576], P(('dp', 'expert')), may hold values from 0 to 575, each once within a row
- projection: float32 [768, 2304], P(('dp', 'expert')), may hold values from -1 to 1
- projection_first: float32 [768, 2304], P(('dp', 'expert'))
- projection_second: float32 [768, 2304], P(('dp', 'expert'))
- output_weight: float32 [768, 768], P(('dp', 'expert')), may hold values from -2.5 to 2.5
- output_first: float32 [768, 768], P(('dp', 'expert'))
- output_second: float32 [768, 768], P(('dp', 'expert'))
- router_weight: float32 [768, 16], P(('dp', 'expert')), may hold values from -0.125 to 0.125
- router_first: float32 [768, 16], P(('dp', 'expert'))
- router_second: float32 [768, 16], P(('dp', 'expert'))
- vectors: float32 [7, 768], P(None, ('dp', 'expert')), may hold values from -0.4 to 2.5
- vectors_first: float32 [7, 768], P(None, ('dp', 'expert'))
- vectors_second: float32 [7, 768], P(None, ('dp', 'expert'))
- expert_inner: float32 [16, 768, 3072], P('expert', None, 'dp'), may hold values from -0.21875 to 0.21875
- inner_first: float32 [16, 768, 3072], P('expert', None, 'dp')
- inner_second: float32 [16, 768, 3072], P('expert', None, 'dp')
- hidden_bias: float32 [16, 3072], P('expert', 'dp'), may hold values from -0.6 to 0.6
- hidden_first: float32 [16, 3072], P('expert', 'dp')
- hidden_second: float32 [16, 3072], P('expert', 'dp')
- expert_outer: float32 [16, 3072, 768], P('expert', 'dp'), may hold values from -1.75 to 1.75
- outer_first: float32 [16, 3072, 768], P('expert', 'dp')
- outer_second: float32 [16, 3072, 768], P('expert', 'dp')
- return_bias: float32 [16, 768], P('expert', 'dp'), may hold values from -6 to 6
- return_first: float32 [16, 768], P('expert', 'dp')
- return_second: float32 [16, 768], P('expert', 'dp')
Outputs:
- block_output: bfloat16 [32, 576, 768], P(('dp', 'expert'))
- input_grad: float32 [32, 576, 768], P(('dp', 'expert'))
- grad_norm: float32 [], replicated
- projection_next: float32 [768, 2304], P(('dp', 'expert'))
- projection_moment: float32 [768, 2304], P(('dp', 'expert'))
- projection_square: float32 [768, 2304], P(('dp', 'expert'))
- output_next: float32 [768, 768], P(('dp', 'expert'))
- output_moment: float32 [768, 768], P(('dp', 'expert'))
- output_square: float32 [768, 768], P(('dp', 'expert'))
- router_next: float32 [768, 16], P(('dp', 'expert'))
- router_moment: float32 [768, 16], P(('dp', 'expert'))
- router_square: float32 [768, 16], P(('dp', 'expert'))
- vectors_next: float32 [7, 768], P(None, ('dp', 'expert'))
- vectors_moment: float32 [7, 768], P(None, ('dp', 'expert'))
- vectors_square: float32 [7, 768], P(None, ('dp', 'expert'))
- inner_next: float32 [16, 768, 3072], P('expert', None, 'dp')
- inner_moment: float32 [16, 768, 3072], P('expert', None, 'dp')
- inner_square: float32 [16, 768, 3072], P('expert', None, 'dp')
- hidden_next: float32 [16, 3072], P('expert', 'dp')
- hidden_moment: float32 [16, 3072], P('expert', 'dp')
- hidden_square: float32 [16, 3072], P('expert', 'dp')
- outer_next: float32 [16, 3072, 768], P('expert', 'dp')
- outer_moment: float32 [16, 3072, 768], P('expert', 'dp')
- outer_square: float32 [16, 3072, 768], P('expert', 'dp')
- return_next: float32 [16, 768], P('expert', 'dp')
- return_moment: float32 [16, 768], P('expert', 'dp')
- return_square: float32 [16, 768], P('expert', 'dp')
Inputs may be any that keep to these rules, and one draw needn't show every extreme that they name: `expert_choice`: the 2 experts of a patch are all different. `priority`: in each image every number from 0 to 575 stands once; a lower number claims expert slots earlier.
All inputs are finite; a program needn't handle non-finite values.
Results may differ from a plain program's by a relative error of at most 0.025.
Values may be sent and summed in bfloat16 or wider, within the bound.
A program may use at most 256 MiB of HBM per device.

v0:
```python
import functools

import jax
import jax.numpy as jnp
from jax import lax
from jax.experimental import pallas as pl
from jax.experimental.pallas import tpu as pltpu
from jax.sharding import PartitionSpec as P

HEADS = 12
HEAD_DIM = 64
STEP = 10


NORM_EPS = 1e-06
ADAM_EPS = 1e-08
BETA_ONE = 0.9
BETA_TWO = 0.999
DECAY = 0.1
THRESHOLD = 1.0
RATE_PROJECTION = 0.1
RATE_OUTPUT = 1.0
RATE_ROUTER = 0.05
RATE_VECTORS = 0.5
RATE_INNER = 0.1
RATE_HIDDEN = 0.25
RATE_OUTER = 1.5
RATE_RETURN = 2.0


def layer_norm(values, norm_gain, norm_bias):
    center = values - jnp.mean(values, axis=-1, keepdims=True)
    spread = jnp.mean(center * center, axis=-1, keepdims=True)
    return center * lax.rsqrt(spread + NORM_EPS) * norm_gain + norm_bias


def smooth_gate(values):
    return jax.nn.gelu(values, approximate=True)


def mixed_dot(left, right):
    return jnp.dot(left, right, preferred_element_type=jnp.float32)


def rows_product(left, right):
    return lax.dot_general(
        left, right, (((0,), (0,)), ((), ())), preferred_element_type=jnp.float32
    )


def columns_product(left, right):
    return lax.dot_general(
        left, right, (((1,), (1,)), ((), ())), preferred_element_type=jnp.float32
    )


def assign_slots(chosen, claim_order, expert_count, capacity):
    patches = chosen.shape[0]
    top_count = chosen.shape[1]
    claim_rank = (
        jnp.arange(top_count, dtype=jnp.int32)[None, :] * patches + claim_order[:, None]
    ).T.reshape(-1)
    flat_choice = chosen.T.reshape(-1)
    onehot = (flat_choice[:, None] == jnp.arange(expert_count, dtype=jnp.int32)[None, :]).astype(
        jnp.float32
    )
    earlier = (claim_rank[None, :] < claim_rank[:, None]).astype(jnp.float32)
    counts = jnp.dot(
        earlier, onehot, precision=lax.Precision.HIGHEST, preferred_element_type=jnp.float32
    )
    position = jnp.sum(counts * onehot, axis=1).astype(jnp.int32).reshape(top_count, patches).T
    kept_mask = position < capacity
    flat_slot = chosen * capacity + jnp.minimum(position, capacity - 1)
    return (flat_slot, kept_mask)


def slot_matches(flat_slot, kept_mask, slot_count):
    slot_ids = jnp.arange(slot_count, dtype=jnp.int32)
    return (flat_slot[None, :, :] == slot_ids[:, None, None]) & kept_mask[None, :, :]


def select_gates(logits, chosen, expert_count):
    router_probs = jax.nn.softmax(logits, axis=-1)
    onehot = chosen[:, :, None] == jnp.arange(expert_count, dtype=jnp.int32)[None, None, :]
    return jnp.sum(jnp.where(onehot, router_probs[:, None, :], 0.0), axis=2)


def adam_update(weight, first_state, second, gradient, clip_factor, step_rate, decay_rate):
    scaled = gradient * clip_factor
    first_new = BETA_ONE * first_state + (1.0 - BETA_ONE) * scaled
    second_new = BETA_TWO * second + (1.0 - BETA_TWO) * scaled * scaled
    first_hat = first_new / (1.0 - BETA_ONE**STEP)
    second_hat = second_new / (1.0 - BETA_TWO**STEP)
    weight_new = weight - step_rate * (
        first_hat / (jnp.sqrt(second_hat) + ADAM_EPS) + decay_rate * weight
    )
    return (weight_new, first_new, second_new)


def shards(
    tokens,
    cotangent,
    expert_choice,
    priority,
    projection,
    projection_first,
    projection_second,
    output_weight,
    output_first,
    output_second,
    router_weight,
    router_first,
    router_second,
    vectors,
    vectors_first,
    vectors_second,
    expert_inner,
    inner_first,
    inner_second,
    hidden_bias,
    hidden_first,
    hidden_second,
    expert_outer,
    outer_first,
    outer_second,
    return_bias,
    return_first,
    return_second,
):
    model_width = tokens.shape[2]
    patches = tokens.shape[1]
    experts = lax.axis_size("expert")
    capacity = max(2, patches // experts)
    slot_count = experts * capacity
    score_scale = HEAD_DIM ** (-0.5)
    dense_shards = (
        projection.astype(jnp.bfloat16),
        output_weight.astype(jnp.bfloat16),
        router_weight.astype(jnp.bfloat16),
        vectors.astype(jnp.bfloat16),
    )
    partial_shards = (
        lax.all_gather(dense_shards[0], "expert", axis=0, tiled=True),
        lax.all_gather(dense_shards[1], "expert", axis=0, tiled=True),
        lax.all_gather(dense_shards[2], "expert", axis=0, tiled=True),
        lax.all_gather(dense_shards[3], "expert", axis=1, tiled=True),
    )
    whole_projection, whole_output, whole_router, whole_vectors = (
        lax.all_gather(partial_shards[0], "dp", axis=0, tiled=True),
        lax.all_gather(partial_shards[1], "dp", axis=0, tiled=True),
        lax.all_gather(partial_shards[2], "dp", axis=0, tiled=True),
        lax.all_gather(partial_shards[3], "dp", axis=1, tiled=True),
    )
    inner_low = expert_inner.astype(jnp.bfloat16)
    hidden_low = hidden_bias.astype(jnp.bfloat16)
    outer_low = expert_outer.astype(jnp.bfloat16)
    return_low = return_bias.astype(jnp.bfloat16)
    inner_all, hidden_all, outer_all, return_all = (
        lax.all_gather(inner_low, "dp", axis=2, tiled=True),
        lax.all_gather(hidden_low, "dp", axis=1, tiled=True),
        lax.all_gather(outer_low, "dp", axis=1, tiled=True),
        lax.all_gather(return_low, "dp", axis=1, tiled=True),
    )
    vector_rows = whole_vectors.astype(jnp.float32)
    image_rows = tokens[0].astype(jnp.float32)
    normed_one, norm_back_one = jax.vjp(layer_norm, image_rows, vector_rows[0], vector_rows[1])
    normed_low = normed_one.astype(jnp.bfloat16)
    projected = mixed_dot(normed_low, whole_projection)
    queries = (
        (projected[:, :model_width] + vector_rows[2])
        .astype(jnp.bfloat16)
        .reshape(patches, HEADS, HEAD_DIM)
    )
    key_rows = (
        projected[:, model_width : 2 * model_width]
        .astype(jnp.bfloat16)
        .reshape(patches, HEADS, HEAD_DIM)
    )
    value_rows = (
        (projected[:, 2 * model_width :] + vector_rows[3])
        .astype(jnp.bfloat16)
        .reshape(patches, HEADS, HEAD_DIM)
    )
    scores = (
        jnp.einsum("qhd,khd->hqk", queries, key_rows, preferred_element_type=jnp.float32)
        * score_scale
    )
    score_top = jnp.max(scores, axis=-1, keepdims=True)
    raised = jnp.exp(scores - score_top)
    totals = jnp.sum(raised, axis=-1, keepdims=True)
    attention = raised / totals
    log_total = score_top + jnp.log(totals)
    context = (
        jnp.einsum(
            "hqk,khd->qhd",
            attention.astype(jnp.bfloat16),
            value_rows,
            preferred_element_type=jnp.float32,
        )
        .reshape(patches, model_width)
        .astype(jnp.bfloat16)
    )
    middle = image_rows + (mixed_dot(context, whole_output) + vector_rows[4])
    normed_two, norm_back_two = jax.vjp(layer_norm, middle, vector_rows[5], vector_rows[6])
    second_low = normed_two.astype(jnp.bfloat16)
    logits = mixed_dot(second_low, whole_router)
    chosen = expert_choice[0]

    def gate_choice(values):
        return select_gates(values, chosen, experts)

    gate_values, gate_back = jax.vjp(gate_choice, logits)
    flat_slot, kept_mask = assign_slots(chosen, priority[0], experts, capacity)
    matches = slot_matches(flat_slot, kept_mask, slot_count)
    slot_table = jnp.any(matches, axis=2).astype(jnp.bfloat16)
    dispatched = (
        mixed_dot(slot_table, second_low)
        .astype(jnp.bfloat16)
        .reshape(experts, capacity, model_width)
    )
    arrived = lax.all_to_all(dispatched, "expert", split_axis=0, concat_axis=0, tiled=True).reshape(
        slot_count, model_width
    )
    pre_act = mixed_dot(arrived, inner_all[0]) + hidden_all[0].astype(jnp.float32)
    activated, gelu_back = jax.vjp(smooth_gate, pre_act)
    active_low = activated.astype(jnp.bfloat16)
    expert_out = (mixed_dot(active_low, outer_all[0]) + return_all[0].astype(jnp.float32)).astype(
        jnp.bfloat16
    )
    returned = lax.all_to_all(
        expert_out.reshape(experts, capacity, model_width),
        "expert",
        split_axis=0,
        concat_axis=0,
        tiled=True,
    ).reshape(slot_count, model_width)
    picked = returned[flat_slot].astype(jnp.float32)
    weighted = jnp.where(kept_mask, gate_values, 0.0)
    final = middle + jnp.sum(weighted[:, :, None] * picked, axis=1)
    block_output = final.astype(jnp.bfloat16)[None]
    upstream = cotangent[0].astype(jnp.float32)
    gate_grad = jnp.where(kept_mask, jnp.sum(upstream[:, None, :] * picked, axis=2), 0.0)
    slot_gate = jnp.sum(jnp.where(matches, weighted[None, :, :], 0.0), axis=(1, 2))
    slot_grad = (mixed_dot(slot_table, cotangent[0]) * slot_gate[:, None]).astype(jnp.bfloat16)
    sent_grad = lax.all_to_all(
        slot_grad.reshape(experts, capacity, model_width),
        "expert",
        split_axis=0,
        concat_axis=0,
        tiled=True,
    ).reshape(slot_count, model_width)
    outer_grad = rows_product(active_low, sent_grad)
    return_grad = jnp.sum(sent_grad, axis=0, dtype=jnp.float32)
    active_grad = columns_product(sent_grad, outer_all[0])
    (pre_grad,) = gelu_back(active_grad)
    pre_low = pre_grad.astype(jnp.bfloat16)
    inner_grad = rows_product(arrived, pre_low)
    hidden_grad = jnp.sum(pre_low, axis=0, dtype=jnp.float32)
    row_grad = columns_product(pre_low, inner_all[0]).astype(jnp.bfloat16)
    expert_grads = (
        lax.psum_scatter(
            inner_grad[None].astype(jnp.bfloat16), "dp", scatter_dimension=2, tiled=True
        ).astype(jnp.float32),
        lax.psum_scatter(
            hidden_grad[None].astype(jnp.bfloat16), "dp", scatter_dimension=1, tiled=True
        ).astype(jnp.float32),
        lax.psum_scatter(
            outer_grad[None].astype(jnp.bfloat16), "dp", scatter_dimension=1, tiled=True
        ).astype(jnp.float32),
        lax.psum_scatter(
            return_grad[None].astype(jnp.bfloat16), "dp", scatter_dimension=1, tiled=True
        ).astype(jnp.float32),
    )
    back_rows = lax.all_to_all(
        row_grad.reshape(experts, capacity, model_width),
        "expert",
        split_axis=0,
        concat_axis=0,
        tiled=True,
    ).reshape(slot_count, model_width)
    (logit_grad,) = gate_back(gate_grad)
    logit_low = logit_grad.astype(jnp.bfloat16)
    router_grad = rows_product(second_low, logit_low)
    second_grad = rows_product(slot_table, back_rows) + columns_product(logit_low, whole_router)
    middle_part, gain_two_grad, bias_two_grad = norm_back_two(second_grad)
    middle_grad = upstream + middle_part
    branch_low = middle_grad.astype(jnp.bfloat16)
    output_grad = rows_product(context, branch_low)
    out_bias_grad = jnp.sum(branch_low, axis=0, dtype=jnp.float32)
    context_grad = (
        columns_product(branch_low, whole_output)
        .astype(jnp.bfloat16)
        .reshape(patches, HEADS, HEAD_DIM)
    )
    scores = (
        jnp.einsum("qhd,khd->hqk", queries, key_rows, preferred_element_type=jnp.float32)
        * score_scale
    )
    attention = jnp.exp(scores - log_total)
    attention_grad = jnp.einsum(
        "qhd,khd->hqk", context_grad, value_rows, preferred_element_type=jnp.float32
    )
    value_grad = jnp.einsum(
        "hqk,qhd->khd",
        attention.astype(jnp.bfloat16),
        context_grad,
        preferred_element_type=jnp.float32,
    ).astype(jnp.bfloat16)
    centered = jnp.sum(attention * attention_grad, axis=-1, keepdims=True)
    score_grad = (attention * (attention_grad - centered)).astype(jnp.bfloat16)
    query_grad = (
        (
            jnp.einsum("hqk,khd->qhd", score_grad, key_rows, preferred_element_type=jnp.float32)
            * score_scale
        )
        .astype(jnp.bfloat16)
        .reshape(patches, model_width)
    )
    key_grad = (
        (
            jnp.einsum("hqk,qhd->khd", score_grad, queries, preferred_element_type=jnp.float32)
            * score_scale
        )
        .astype(jnp.bfloat16)
        .reshape(patches, model_width)
    )
    value_flat = value_grad.reshape(patches, model_width)
    joined_grad = jnp.concatenate([query_grad, key_grad, value_flat], axis=1)
    projection_grad = rows_product(normed_low, joined_grad)
    normed_grad = columns_product(joined_grad, whole_projection)
    input_part, gain_one_grad, bias_one_grad = norm_back_one(normed_grad)
    input_grad = (middle_grad + input_part)[None]
    vector_grad = jnp.stack(
        [
            gain_one_grad,
            bias_one_grad,
            jnp.sum(query_grad, axis=0, dtype=jnp.float32),
            jnp.sum(value_flat, axis=0, dtype=jnp.float32),
            out_bias_grad,
            gain_two_grad,
            bias_two_grad,
        ]
    )
    local_grads = (projection_grad, output_grad, router_grad, vector_grad)
    partial_grads = (
        lax.psum_scatter(
            local_grads[0].astype(jnp.bfloat16), "dp", scatter_dimension=0, tiled=True
        ).astype(jnp.float32),
        lax.psum_scatter(
            local_grads[1].astype(jnp.bfloat16), "dp", scatter_dimension=0, tiled=True
        ).astype(jnp.float32),
        lax.psum_scatter(
            local_grads[2].astype(jnp.bfloat16), "dp", scatter_dimension=0, tiled=True
        ).astype(jnp.float32),
        lax.psum_scatter(
            local_grads[3].astype(jnp.bfloat16), "dp", scatter_dimension=1, tiled=True
        ).astype(jnp.float32),
    )
    dense_grads = (
        lax.psum_scatter(
            partial_grads[0].astype(jnp.bfloat16), "expert", scatter_dimension=0, tiled=True
        ).astype(jnp.float32),
        lax.psum_scatter(
            partial_grads[1].astype(jnp.bfloat16), "expert", scatter_dimension=0, tiled=True
        ).astype(jnp.float32),
        lax.psum_scatter(
            partial_grads[2].astype(jnp.bfloat16), "expert", scatter_dimension=0, tiled=True
        ).astype(jnp.float32),
        lax.psum_scatter(
            partial_grads[3].astype(jnp.bfloat16), "expert", scatter_dimension=1, tiled=True
        ).astype(jnp.float32),
    )
    all_grads = tuple(dense_grads) + tuple(expert_grads)
    local_square = jnp.sum(all_grads[0] * all_grads[0])
    for gradient in all_grads[1:]:
        local_square = local_square + jnp.sum(gradient * gradient)
    square_total = lax.psum(local_square, ("dp", "expert"))
    grad_norm = jnp.sqrt(square_total)
    clip_factor = THRESHOLD / jnp.maximum(grad_norm, THRESHOLD)
    projection_next, projection_moment, projection_square = adam_update(
        projection,
        projection_first,
        projection_second,
        all_grads[0],
        clip_factor,
        RATE_PROJECTION,
        DECAY,
    )
    output_next, output_moment, output_square = adam_update(
        output_weight, output_first, output_second, all_grads[1], clip_factor, RATE_OUTPUT, DECAY
    )
    router_next, router_moment, router_square = adam_update(
        router_weight, router_first, router_second, all_grads[2], clip_factor, RATE_ROUTER, DECAY
    )
    vectors_next, vectors_moment, vectors_square = adam_update(
        vectors, vectors_first, vectors_second, all_grads[3], clip_factor, RATE_VECTORS, 0.0
    )
    inner_next, inner_moment, inner_square = adam_update(
        expert_inner, inner_first, inner_second, all_grads[4], clip_factor, RATE_INNER, DECAY
    )
    hidden_next, hidden_moment, hidden_square = adam_update(
        hidden_bias, hidden_first, hidden_second, all_grads[5], clip_factor, RATE_HIDDEN, 0.0
    )
    outer_next, outer_moment, outer_square = adam_update(
        expert_outer, outer_first, outer_second, all_grads[6], clip_factor, RATE_OUTER, DECAY
    )
    return_next, return_moment, return_square = adam_update(
        return_bias, return_first, return_second, all_grads[7], clip_factor, RATE_RETURN, 0.0
    )
    return (
        block_output,
        input_grad,
        grad_norm,
        projection_next,
        projection_moment,
        projection_square,
        output_next,
        output_moment,
        output_square,
        router_next,
        router_moment,
        router_square,
        vectors_next,
        vectors_moment,
        vectors_square,
        inner_next,
        inner_moment,
        inner_square,
        hidden_next,
        hidden_moment,
        hidden_square,
        outer_next,
        outer_moment,
        outer_square,
        return_next,
        return_moment,
        return_square,
    )


MESH = pl.DeviceIdType.MESH
ANY = pl.BlockSpec(memory_space=pl.ANY)
VMEM = pl.BlockSpec(memory_space=pltpu.VMEM)


class Place:
    def __init__(self, dp, experts):
        self.dp, self.experts = dp, experts
        self.ys = 2
        self.zs = experts // 4
        self.a = lax.axis_index("dp")
        self.e = lax.axis_index("expert")
        self.core = lax.rem(self.e, 2)
        self.y = lax.rem(lax.div(self.e, 2), self.ys)
        self.z = lax.div(self.e, 2 * self.ys)

    def chip_of(self, core, dz, s2, s3):
        zz = lax.rem(self.z + dz, self.zs)
        if s2 == s3:
            fa = fy = s2
        elif s2:
            fa, fy = core, 1 - core
        else:
            fa, fy = 1 - core, core
        aa = lax.rem(self.a + fa, 2)
        yy = lax.rem(self.y + fy, 2)
        return aa, zz, yy

    def device(self, core, dz, s2, s3, own_core=None):
        aa, zz, yy = self.chip_of(core, dz, s2, s3)
        c = core if own_core is None else own_core
        return (aa, (zz * self.ys + yy) * 2 + c)

    def flat(self, dev):
        return dev[0] * self.experts + dev[1]

    def chip(self, core, dz, s2, s3):
        aa, zz, yy = self.chip_of(core, dz, s2, s3)
        return (aa * self.zs + zz) * self.ys + yy


def remote(src, dst, send, recv, dev):
    return pltpu.make_async_remote_copy(src_ref=src, dst_ref=dst, send_sem=send, recv_sem=recv, device_id=dev, device_id_type=MESH)


def greet(devices):
    barrier = pltpu.get_barrier_semaphore()
    for dev in devices:
        pl.semaphore_signal(barrier, inc=1, device_id=dev, device_id_type=MESH)
    pl.semaphore_wait(barrier, len(devices))


def split_index(k, zs):
    return k % zs, (k // zs) % 2, k // (2 * zs)


def gather_kernel(dp, experts, in_ref, out_ref, send, recv, csend, crecv, own):
    p = Place(dp, experts)
    zs = p.zs
    c = p.core
    n = 4 * zs
    partner = (p.a, p.e + 1 - 2 * c)
    peers = [p.device(c, dz, 0, 0) for dz in range(1, zs)]
    second = p.device(c, 0, 1, 0)
    third = p.device(c, 0, 0, 1)
    me = p.flat((p.a, p.e))
    mine = pltpu.make_async_copy(in_ref, out_ref.at[me], own)
    mine.start()
    greet(peers + [second, third, partner])
    pending = []

    def block(k):
        if k == 0:
            return me, in_ref
        dz, s2, s3 = split_index(k, zs)
        at = p.flat(p.device(c, (zs - dz) % zs, s2, s3))
        return at, out_ref.at[at]

    def push(k, slot, dev):
        at, src = block(k)
        cp = remote(src, out_ref.at[at], send.at[slot], recv.at[slot], dev)
        cp.start()
        pending.append(cp)

    def hand(k):
        at, src = block(k)
        cp = remote(src, out_ref.at[at], csend.at[k], crecv.at[k], partner)
        cp.start()
        pending.append(cp)

    def arrived(k):
        at, _ = block(k)
        remote(in_ref, out_ref.at[at], send.at[k], recv.at[k], partner).wait_recv()

    for dz in range(1, zs):
        push(0, dz, peers[dz - 1])
    push(0, zs, second)
    push(0, 2 * zs, third)
    hand(0)
    for k in range(1, zs):
        arrived(k)
        push(k, zs + k, second)
        push(k, 2 * zs + k, third)
        hand(k)
    for k in range(zs, 2 * zs):
        arrived(k)
        push(k, 2 * zs + k, third)
        hand(k)
    for k in range(2 * zs, 4 * zs):
        arrived(k)
        hand(k)
    for k in range(n):
        dz, s2, s3 = split_index(k, zs)
        at = p.flat(p.device(1 - c, (zs - dz) % zs, s2, s3))
        remote(in_ref, out_ref.at[at], csend.at[k], crecv.at[k], partner).wait_recv()
    for cp in pending:
        cp.wait_send()
    mine.wait()


def gather_blocks(block, dp, experts, cid):
    n = dp * experts
    return pl.pallas_call(
        functools.partial(gather_kernel, dp, experts),
        out_shape=jax.ShapeDtypeStruct((n,) + block.shape, block.dtype),
        in_specs=[ANY],
        out_specs=ANY,
        scratch_shapes=[
            pltpu.SemaphoreType.DMA((n // 2,)),
            pltpu.SemaphoreType.DMA((n // 2,)),
            pltpu.SemaphoreType.DMA((n // 2,)),
            pltpu.SemaphoreType.DMA((n // 2,)),
            pltpu.SemaphoreType.DMA,
        ],
        compiler_params=pltpu.CompilerParams(collective_id=cid, has_side_effects=True),
        name="gather_dense",
    )(block)


def reduce_kernel(dp, experts, grad_ref, part_ref, out_ref, total_ref, own, rc, r3, r2, rz, fin, row, tiles,
                  load, csend, crecv, send, recv, fsend, frecv, nsend, nrecv):
    p = Place(dp, experts)
    zs = p.zs
    c = p.core
    n = 4 * zs
    world = dp * experts
    half = own.shape[2]
    deep = own.shape[1] // 2
    partner = (p.a, p.e + 1 - 2 * c)
    second = p.device(c, 0, 1, 0)
    third = p.device(c, 0, 0, 1)
    me = p.flat((p.a, p.e))
    everyone = []
    for j in range(1, world):
        other = lax.rem(me + j, world)
        everyone.append((lax.div(other, experts), lax.rem(other, experts)))
    mycols = pl.ds(pl.multiple_of(c * half, 128), half)
    hiscols = pl.ds(pl.multiple_of((1 - c) * half, 128), half)
    order = list(range(2 * zs, n)) + list(range(zs, 2 * zs)) + list(range(1, zs)) + [0]
    loads = {}
    for k in order:
        loads[k] = pltpu.make_async_copy(grad_ref.at[p.chip(c, *split_index(k, zs)), :, mycols], own.at[k], load.at[k])
        loads[k].start()
    greet(everyone)
    pending = []

    def push(src, dst, ss, rs, dev):
        cp = remote(src, dst, ss, rs, dev)
        cp.start()
        pending.append(cp)

    for k in order:
        push(grad_ref.at[p.chip(1 - c, *split_index(k, zs)), :, hiscols], rc.at[k], csend.at[k], crecv.at[k], partner)

    def got(ref, sem):
        remote(ref, ref, sem, sem, partner).wait_recv()

    for k in order:
        loads[k].wait()
        got(rc.at[k], crecv.at[k])
        total = own[k].astype(jnp.float32) + rc[k].astype(jnp.float32)
        if k < 2 * zs:
            got(r3.at[k], recv.at[2 * zs + k])
            total = total + r3[k].astype(jnp.float32)
        if k < zs:
            got(r2.at[k], recv.at[zs + k])
            total = total + r2[k].astype(jnp.float32)
        if k >= 1:
            own[k] = total.astype(own.dtype)
        if k >= 2 * zs:
            push(own.at[k], r3.at[k - 2 * zs], send.at[k], recv.at[k], third)
        elif k >= zs:
            push(own.at[k], r2.at[k - zs], send.at[k], recv.at[k], second)
        elif k >= 1:
            push(own.at[k], rz.at[k - 1], send.at[k], recv.at[k], p.device(c, k, 0, 0))
        else:
            for j in range(1, zs):
                got(rz.at[j - 1], recv.at[j])
                total = total + rz[j - 1].astype(jnp.float32)
            fin[...] = total
    his = pl.ds(pl.multiple_of((1 - c) * deep, 8), deep)
    mine = pl.ds(pl.multiple_of(c * deep, 8), deep)
    push(fin.at[his], row, fsend, frecv, partner)
    square = part_ref[...]
    for i in range(2 * deep // 8):
        for j in range(half // 128):
            v = fin[pl.ds(8 * i, 8), pl.ds(128 * j, 128)]
            square = square + v * v
    tiles[me] = square
    for j in range(1, world):
        push(tiles.at[me], tiles.at[me], nsend.at[j], nrecv.at[j], everyone[j - 1])
    out_ref[:, mycols] = fin[mine, :]
    got(row, frecv)
    out_ref[:, hiscols] = row[...]
    for j in range(1, world):
        src = lax.rem(me + world - j, world)
        got(tiles.at[src], nrecv.at[j])
    total = tiles[0]
    for j in range(1, world):
        total = total + tiles[j]
    total_ref[...] = total
    for cp in pending:
        cp.wait_send()


def reduce_blocks(grads, part, dp, experts, cid):
    n = dp * experts
    chips, rows, cols = grads.shape
    half = cols // 2
    bf = jnp.bfloat16
    return pl.pallas_call(
        functools.partial(reduce_kernel, dp, experts),
        out_shape=[jax.ShapeDtypeStruct((rows // 2, cols), jnp.float32), jax.ShapeDtypeStruct((8, 128), jnp.float32)],
        in_specs=[ANY, VMEM],
        out_specs=[VMEM, VMEM],
        scratch_shapes=[
            pltpu.VMEM((chips, rows, half), bf),
            pltpu.VMEM((chips, rows, half), bf),
            pltpu.VMEM((chips // 2, rows, half), bf),
            pltpu.VMEM((chips // 4, rows, half), bf),
            pltpu.VMEM((chips // 4 - 1, rows, half), bf),
            pltpu.VMEM((rows, half), jnp.float32),
            pltpu.VMEM((rows // 2, half), jnp.float32),
            pltpu.VMEM((n, 8, 128), jnp.float32),
            pltpu.SemaphoreType.DMA((chips,)),
            pltpu.SemaphoreType.DMA((chips,)),
            pltpu.SemaphoreType.DMA((chips,)),
            pltpu.SemaphoreType.DMA((chips,)),
            pltpu.SemaphoreType.DMA((chips,)),
            pltpu.SemaphoreType.DMA,
            pltpu.SemaphoreType.DMA,
            pltpu.SemaphoreType.DMA((n,)),
            pltpu.SemaphoreType.DMA((n,)),
        ],
        compiler_params=pltpu.CompilerParams(collective_id=cid, has_side_effects=True, vmem_limit_bytes=32 * 1024 * 1024),
        name="reduce_dense",
    )(grads, part)


LANES = 128


def nn(left, right):
    return lax.dot_general(left, right, (((1,), (0,)), ((), ())), preferred_element_type=jnp.float32)


def nt(left, right):
    return lax.dot_general(left, right, (((1,), (1,)), ((), ())), preferred_element_type=jnp.float32)


def lane_ids(rows, start=0):
    return lax.broadcasted_iota(jnp.int32, (rows, LANES), 1) + start


def row_parts(count, size):
    return [pl.ds(i * size, size) for i in range(count // size)]


def norm_parts(values):
    center = values - jnp.mean(values, axis=-1, keepdims=True)
    inverse = lax.rsqrt(jnp.mean(center * center, axis=-1, keepdims=True) + NORM_EPS)
    return center * inverse, inverse


def vector_table(weights, width):
    return jnp.transpose(weights[:, 4 * width :].astype(jnp.float32))


def forward_kernel(
    experts,
    capacity,
    chunk,
    tok_ref,
    cot_ref,
    choice_ref,
    rank_col,
    rank_row,
    weights_any,
    rows_ref,
    dy_ref,
    qkv_ref,
    ctx_ref,
    mid_ref,
    second_ref,
    stat_ref,
    aux_ref,
    probs_ref,
    weights,
    vec,
    normed,
    load,
):
    low = jnp.bfloat16
    patches, width = tok_ref.shape
    fetch = pltpu.make_async_copy(weights_any, weights, load)
    fetch.start()
    lanes = lane_ids(patches)
    first, other = choice_ref[:, 0:1], choice_ref[:, 1:2]
    is_first, is_other = lanes == first, lanes == other
    before = (rank_row[...] < rank_col[...]).astype(jnp.float32).astype(low)
    hot = (is_first | (lanes == other + experts)).astype(jnp.float32)
    counts = nn(before, hot.astype(low))
    totals = jnp.sum(hot, axis=0, keepdims=True)
    place_first = jnp.sum(jnp.where(is_first, counts, 0.0), axis=1, keepdims=True)
    place_other = jnp.sum(
        jnp.where(lanes == other + experts, counts, 0.0) + jnp.where(is_other, totals, 0.0), axis=1, keepdims=True
    )
    fetch.wait()
    vec[...] = vector_table(weights, width)

    def row(i):
        return vec[experts + i : experts + i + 1, :]

    for part in row_parts(patches, chunk):
        unit, _ = norm_parts(tok_ref[part, :].astype(jnp.float32))
        normed[part, :] = (unit * row(0) + row(1)).astype(low)
    third = 256
    for base, bias in ((0, 2), (width, None), (2 * width, 3)):
        for j in range(width // third):
            columns = pl.ds(base + j * third, third)
            product = nn(normed[...], weights[:, columns])
            if bias is not None:
                product = product + vec[experts + bias : experts + bias + 1, pl.ds(j * third, third)]
            qkv_ref[:, columns] = product.astype(low)
    stat_ref[...] = jnp.zeros_like(stat_ref)

    @pl.loop(0, width // LANES)
    def _(pair):
        at = pl.multiple_of(pair * LANES, LANES)
        keys = qkv_ref[:, pl.ds(pl.multiple_of(width + at, LANES), LANES)]
        values = qkv_ref[:, pl.ds(pl.multiple_of(2 * width + at, LANES), LANES)]
        key_lanes = lane_ids(patches)
        values_two = [
            jnp.where(key_lanes < HEAD_DIM, values, (key_lanes == HEAD_DIM).astype(jnp.float32).astype(low)),
            jnp.where(key_lanes >= HEAD_DIM, values, (key_lanes == 0).astype(jnp.float32).astype(low)),
        ]
        for part in row_parts(patches, chunk):
            own = lane_ids(chunk)
            queries = qkv_ref[part, pl.ds(at, LANES)] * jnp.asarray(HEAD_DIM**-0.5, low)
            outs = []
            stat = stat_ref[part, :]
            for head in range(2):
                mine = (own < HEAD_DIM) if head == 0 else (own >= HEAD_DIM)
                scores = nt(jnp.where(mine, queries, jnp.zeros_like(queries)), keys)
                top = jnp.max(scores, axis=1, keepdims=True)
                raised = jnp.exp(scores - top)
                mixed = nn(raised.astype(low), values_two[head])
                spare = HEAD_DIM if head == 0 else 0
                total = mixed[:, spare : spare + 1]
                outs.append(mixed / total)
                stat = jnp.where(own == 2 * pair + head, top + jnp.log(total), stat)
            stat_ref[part, :] = stat
            ctx_ref[part, pl.ds(at, LANES)] = jnp.where(own < HEAD_DIM, outs[0], outs[1]).astype(low)

    for j in range(width // third):
        columns = pl.ds(j * third, third)
        product = nn(ctx_ref[...], weights[:, pl.ds(3 * width + j * third, third)])
        mid_ref[:, columns] = tok_ref[:, columns].astype(jnp.float32) + (
            product + vec[experts + 4 : experts + 5, columns]
        )
    for part in row_parts(patches, chunk):
        unit, _ = norm_parts(mid_ref[part, :])
        second_ref[part, :] = (unit * row(5) + row(6)).astype(low)
    logits = jnp.where(lanes < experts, nn(second_ref[...], weights[:, 4 * width :]), -1e30)
    raised = jnp.exp(logits - jnp.max(logits, axis=1, keepdims=True))
    probs = raised / jnp.sum(raised, axis=1, keepdims=True)
    probs_ref[...] = probs

    def slot_of(place, expert):
        place = place.astype(jnp.int32)
        kept = place < capacity
        slot = (place // 8) * LANES + expert * 8 + place % 8
        tail = kept & (place >= capacity - 4)
        return kept, jnp.where(kept, slot, -1), jnp.where(tail, slot + 4, -1)

    aux = jnp.zeros((patches, LANES), jnp.float32)
    for j, (place, expert, hit) in enumerate(((place_first, first, is_first), (place_other, other, is_other))):
        kept, slot, twin = slot_of(place, expert)
        gate = jnp.where(kept, jnp.sum(jnp.where(hit, probs, 0.0), axis=1, keepdims=True), 0.0)
        for lane, column in ((j, slot.astype(jnp.float32)), (2 + j, twin.astype(jnp.float32)), (4 + j, gate)):
            aux = jnp.where(lanes == lane, column, aux)
    aux_ref[...] = aux
    turned = jnp.transpose(aux)
    slots = [turned[i : i + 1, :] for i in range(4)]
    gates = [turned[4 + i : 5 + i, :] for i in range(2)]
    full = capacity // 8
    for i in range(full + 1):
        ids = (lax.broadcasted_iota(jnp.int32, (LANES, patches), 0) + i * LANES).astype(jnp.float32)
        hits = [ids == slots[0], ids == slots[1]]
        if i == full:
            hits = [hits[0] | (ids == slots[2]), hits[1] | (ids == slots[3])]
        table = (hits[0] | hits[1]).astype(jnp.float32).astype(low)
        gate = jnp.sum(
            jnp.where(hits[0], gates[0], 0.0) + jnp.where(hits[1], gates[1], 0.0), axis=1, keepdims=True
        )
        sent = nn(table, second_ref[...])
        back = nn(table, cot_ref[...]) * gate
        columns = pl.ds(i * width, width)
        if i == full:
            columns = pl.ds(i * width, width // 2)
            left = lax.broadcasted_iota(jnp.int32, (LANES, width // 2), 0) % 8 < 4
            sent = jnp.where(left, sent[:, : width // 2], sent[:, width // 2 :])
            back = jnp.where(left, back[:, : width // 2], back[:, width // 2 :])
        rows_ref[:, columns] = sent.astype(low)
        dy_ref[:, columns] = back.astype(low)


def forward(tokens, cotangent, choice, priority, weights, experts, capacity, chunk=192):
    patches, width = tokens.shape
    low, full = jnp.bfloat16, jnp.float32
    packed = (8 * experts, capacity * width // 8)
    shapes = [
        (packed, low),
        (packed, low),
        ((patches, 3 * width), low),
        ((patches, width), low),
        ((patches, width), full),
        ((patches, width), low),
        ((patches, LANES), full),
        ((patches, LANES), full),
        ((patches, LANES), full),
    ]
    return pl.pallas_call(
        functools.partial(forward_kernel, experts, capacity, chunk),
        out_shape=[jax.ShapeDtypeStruct(*s) for s in shapes],
        in_specs=[VMEM] * 5 + [ANY],
        out_specs=[VMEM] * 9,
        scratch_shapes=[
            pltpu.VMEM(weights.shape, low),
            pltpu.VMEM((LANES, width), full),
            pltpu.VMEM((patches, width), low),
            pltpu.SemaphoreType.DMA,
        ],
        compiler_params=pltpu.CompilerParams(vmem_limit_bytes=56 * 1024 * 1024),
        cost_estimate=pl.CostEstimate(flops=6 * 10**9, bytes_accessed=20 * 10**6, transcendentals=4 * 10**6),
        name="attend_forward",
    )(tokens, cotangent, choice, priority.reshape(patches, 1), priority.reshape(1, patches), weights)


def gelu_both(z):
    root = 0.7978845608028654
    square = z * z
    slope = jnp.tanh(root * z * (1.0 + 0.044715 * square))
    half = 0.5 * (1.0 + slope)
    act = z * half
    grad = half + 0.5 * z * (1.0 - slope * slope) * (root * (1.0 + 3 * 0.044715 * square))
    return act, grad


def tail_picks(count, right):
    rows = lax.broadcasted_iota(jnp.int32, (count // 2, count), 0)
    ids = lax.broadcasted_iota(jnp.int32, (count // 2, count), 1)
    hit = ids == (rows // 4) * 8 + rows % 4 + (4 if right else 0)
    return hit.astype(jnp.float32).astype(jnp.bfloat16)


def backward_kernel(
    experts,
    capacity,
    chunk,
    tok_ref,
    cot_ref,
    choice_ref,
    ret_ref,
    back_ref,
    aux_ref,
    probs_ref,
    mid_ref,
    second_ref,
    ctx_ref,
    stat_ref,
    qkv_ref,
    weights_any,
    out_ref,
    input_ref,
    grad_ref,
    weights,
    vec,
    stacked,
    normed,
    branch,
    dctx,
    joined,
    turned_query,
    dmid,
    work,
    sums,
    load,
):
    low = jnp.bfloat16
    patches, width = tok_ref.shape
    fetch = pltpu.make_async_copy(weights_any, weights, load)
    fetch.start()
    full = capacity // 8
    half = width // 2
    lanes = lane_ids(patches)
    aux = aux_ref[...]
    slots = [aux[:, i : i + 1] for i in range(4)]
    gates = [aux[:, 4 + i : 5 + i] for i in range(2)]
    ids = lax.broadcasted_iota(jnp.int32, (patches, full * LANES), 1).astype(jnp.float32)
    tail_ids = lane_ids(patches, full * LANES).astype(jnp.float32)
    hits = [ids == slots[0], ids == slots[1]]
    lefts = [tail_ids == slots[0], tail_ids == slots[1]]
    rights = [tail_ids == slots[2], tail_ids == slots[3]]

    def mix(marks):
        return (jnp.where(marks[0], gates[0], 0.0) + jnp.where(marks[1], gates[1], 0.0)).astype(low)

    def pick(marks):
        return (marks[0] | marks[1]).astype(jnp.float32).astype(low)

    for i in range(full):
        stacked[pl.ds(i * LANES, LANES), :] = ret_ref[:, pl.ds(i * width, width)]
    tail = ret_ref[:, pl.ds(full * width, half)]
    left_mix, right_mix = nn(mix(lefts), tail), nn(mix(rights), tail)
    final = nn(mix(hits), stacked[...])
    out_ref[:, :half] = (mid_ref[:, :half] + (final[:, :half] + left_mix)).astype(low)
    out_ref[:, half:] = (mid_ref[:, half:] + (final[:, half:] + right_mix)).astype(low)
    along = nt(cot_ref[...], stacked[...])
    along_left, along_right = nt(cot_ref[:, :half], tail), nt(cot_ref[:, half:], tail)
    dprobs = jnp.zeros((patches, LANES), jnp.float32)
    for j in range(2):
        dgate = jnp.sum(jnp.where(hits[j], along, 0.0), axis=1, keepdims=True) + jnp.sum(
            jnp.where(lefts[j], along_left, 0.0) + jnp.where(rights[j], along_right, 0.0), axis=1, keepdims=True
        )
        dprobs = dprobs + jnp.where(lanes == choice_ref[:, j : j + 1], dgate, 0.0)
    probs = probs_ref[...]
    dlogits = (probs * (dprobs - jnp.sum(probs * dprobs, axis=1, keepdims=True))).astype(low)
    for i in range(full):
        stacked[pl.ds(i * LANES, LANES), :] = back_ref[:, pl.ds(i * width, width)]
    tail = back_ref[:, pl.ds(full * width, half)]
    fetch.wait()
    vec[...] = vector_table(weights, width)

    def row(i):
        return vec[experts + i : experts + i + 1, :]

    routed = weights[:, 4 * width :]
    work[...] = nn(pick(hits), stacked[...]) + nt(dlogits, routed)
    work[:, :half] = work[:, :half] + nn(pick(lefts), tail)
    work[:, half:] = work[:, half:] + nn(pick(rights), tail)
    sums[...] = jnp.zeros_like(sums)

    def column_sum(slot, values):
        sums[pl.ds(8 * slot, 8), :] = sums[pl.ds(8 * slot, 8), :] + jnp.sum(
            values.reshape(-1, 8, values.shape[-1]), axis=0
        )

    def norm_back(grad, unit, inverse, gain):
        weighted = grad * gain
        return inverse * (
            weighted
            - jnp.mean(weighted, axis=-1, keepdims=True)
            - unit * jnp.mean(weighted * unit, axis=-1, keepdims=True)
        )

    for part in row_parts(patches, chunk):
        unit, inverse = norm_parts(mid_ref[part, :])
        grad = work[part, :]
        column_sum(5, grad * unit)
        column_sum(6, grad)
        total = cot_ref[part, :].astype(jnp.float32) + norm_back(grad, unit, inverse, row(5))
        dmid[part, :] = total
        rounded = total.astype(low)
        branch[part, :] = rounded
        column_sum(4, rounded.astype(jnp.float32))
    third = 256
    for j in range(width // third):
        rows = pl.ds(j * third, third)
        dctx[:, rows] = nt(branch[...], weights[rows, pl.ds(3 * width, width)]).astype(low)
    second_turned = jnp.transpose(second_ref[...])
    router_grad = nn(second_turned, dlogits)
    ctx_turned = jnp.transpose(ctx_ref[...])
    for j in range(width // third):
        columns = pl.ds(j * third, third)
        grad_ref[:, pl.ds(3 * width + j * third, third)] = nn(ctx_turned, branch[:, columns]).astype(low)
    heads = (
        lax.broadcasted_iota(jnp.int32, (16, width), 1) // HEAD_DIM == lax.broadcasted_iota(jnp.int32, (16, width), 0)
    ).astype(jnp.float32).astype(low)
    product = dctx[...].astype(jnp.float32) * ctx_ref[...].astype(jnp.float32)
    upper = product.astype(low)
    center = nt(heads, upper) + nt(heads, (product - upper.astype(jnp.float32)).astype(low))
    logs = jnp.transpose(stat_ref[...])
    sums_rows = jnp.concatenate([logs[:16], center], axis=0)
    vec_rows = work
    vec_rows[0:32, :patches] = sums_rows

    @pl.loop(0, width // LANES)
    def _(pair):
        at = pl.multiple_of(pair * LANES, LANES)
        key_at = pl.ds(pl.multiple_of(width + at, LANES), LANES)
        value_at = pl.ds(pl.multiple_of(2 * width + at, LANES), LANES)
        scale = jnp.asarray(HEAD_DIM**-0.5, low)
        queries = qkv_ref[:, pl.ds(at, LANES)] * scale
        given = dctx[:, pl.ds(at, LANES)]
        own = lane_ids(patches)
        zero = jnp.zeros_like(queries)
        marks = [own < HEAD_DIM, own >= HEAD_DIM]
        head_queries = [jnp.where(m, queries, zero) for m in marks]
        head_given = [jnp.where(m, given, zero) for m in marks]
        turned_keys = jnp.transpose(qkv_ref[:, key_at] * scale)
        query_parts = [None, None]
        for part in row_parts(patches, chunk):
            keys = qkv_ref[part, key_at]
            values = qkv_ref[part, value_at]
            value_out, key_out = [], []
            for head in range(2):
                log_row = work[pl.ds(2 * pair + head, 1), :patches]
                center_row = work[pl.ds(16 + 2 * pair + head, 1), :patches]
                prob = jnp.exp(nt(keys, head_queries[head]) - log_row)
                value_out.append(nn(prob.astype(low), given))
                dscore = (prob * (nt(values, head_given[head]) - center_row)).astype(low)
                key_out.append(nn(dscore, queries))
                piece = nn(turned_keys[HEAD_DIM * head : HEAD_DIM * (head + 1), part.start : part.start + part.size], dscore)
                query_parts[head] = piece if query_parts[head] is None else query_parts[head] + piece
            side = lane_ids(chunk) < HEAD_DIM
            joined[part, key_at] = jnp.where(side, key_out[0], key_out[1]).astype(low)
            joined[part, value_at] = jnp.where(side, value_out[0], value_out[1]).astype(low)
        turned_query[...] = jnp.concatenate(query_parts, axis=0)
        joined[:, pl.ds(at, LANES)] = jnp.transpose(turned_query[...]).astype(low)

    for part in row_parts(patches, chunk):
        unit, _ = norm_parts(tok_ref[part, :].astype(jnp.float32))
        normed[part, :] = (unit * row(0) + row(1)).astype(low)
        column_sum(2, joined[part, :width].astype(jnp.float32))
        column_sum(3, joined[part, 2 * width :].astype(jnp.float32))
    normed_turned = jnp.transpose(normed[...])
    for j in range(3 * width // third):
        columns = pl.ds(j * third, third)
        grad_ref[:, columns] = nn(normed_turned, joined[:, columns]).astype(low)
    for j in range(width // third):
        rows = pl.ds(j * third, third)
        work[:, rows] = nt(joined[...], weights[rows, : 3 * width])
    for part in row_parts(patches, chunk):
        unit, inverse = norm_parts(tok_ref[part, :].astype(jnp.float32))
        grad = work[part, :]
        column_sum(0, grad * unit)
        column_sum(1, grad)
        input_ref[part, :] = dmid[part, :] + norm_back(grad, unit, inverse, row(0))
    vec[...] = jnp.zeros_like(vec)
    for i in range(7):
        vec[experts + i : experts + i + 1, :] = jnp.sum(sums[pl.ds(8 * i, 8), :], axis=0, keepdims=True)
    last = router_grad + jnp.transpose(vec[...])
    grad_ref[:, pl.ds(4 * width, LANES)] = last.astype(low)
    rest = grad_ref.shape[1] - 4 * width - LANES
    grad_ref[:, pl.ds(4 * width + LANES, rest)] = jnp.zeros((width, rest), low)


def backward(
    tokens, cotangent, choice, ret, back, aux, probs, mid, second, ctx, stat, qkv, weights, experts, capacity, chunk=192
):
    patches, width = tokens.shape
    low, full = jnp.bfloat16, jnp.float32
    columns = -(-weights.shape[1] // 256) * 256
    return pl.pallas_call(
        functools.partial(backward_kernel, experts, capacity, chunk),
        out_shape=[
            jax.ShapeDtypeStruct((patches, width), low),
            jax.ShapeDtypeStruct((patches, width), full),
            jax.ShapeDtypeStruct((width, columns), low),
        ],
        in_specs=[VMEM] * 12 + [ANY],
        out_specs=[VMEM] * 3,
        scratch_shapes=[
            pltpu.VMEM(weights.shape, low),
            pltpu.VMEM((LANES, width), full),
            pltpu.VMEM((capacity // 8 * LANES, width), low),
            pltpu.VMEM((patches, width), low),
            pltpu.VMEM((patches, width), low),
            pltpu.VMEM((patches, width), low),
            pltpu.VMEM((patches, 3 * width), low),
            pltpu.VMEM((LANES, patches), full),
            pltpu.VMEM((patches, width), full),
            pltpu.VMEM((patches, width), full),
            pltpu.VMEM((56, width), full),
            pltpu.SemaphoreType.DMA,
        ],
        compiler_params=pltpu.CompilerParams(vmem_limit_bytes=60 * 1024 * 1024),
        cost_estimate=pl.CostEstimate(flops=15 * 10**9, bytes_accessed=30 * 10**6, transcendentals=4 * 10**6),
        name="attend_backward",
    )(tokens, cotangent, choice, ret, back, aux, probs, mid, second, ctx, stat, qkv, weights)


def moe_kernel(
    dp,
    experts,
    chunk,
    rows_any,
    dy_any,
    inner_any,
    hidden_ref,
    outer_any,
    return_ref,
    y_any,
    drows_any,
    dinner_any,
    dhidden_ref,
    douter_any,
    dreturn_ref,
    square_ref,
    rows_all,
    dy_all,
    y_pack,
    drows_pack,
    y_theirs,
    drows_theirs,
    rows,
    turned,
    dy,
    inner,
    outer,
    act,
    grad,
    dz,
    acc,
    inner_stage,
    outer_stage,
    dinner_stage,
    douter_stage,
    square,
    own_sem,
    in_send,
    in_recv,
    over_send,
    over_recv,
    part_send,
    part_recv,
    out_send,
    out_recv,
    stage_sem,
    store_sem,
):
    low, full32 = jnp.bfloat16, jnp.float32
    width = rows.shape[1]
    count = dp * experts * 8
    half = width // 2
    full = rows_all.shape[3] // width
    steps = inner.shape[1] // chunk
    each = -(-(experts - 1) // (steps - 1))
    a = lax.axis_index("dp")
    e = lax.axis_index("expert")
    across = (1 - a, e)
    ins, alls = (rows_any, dy_any), (rows_all, dy_all)
    packs, theirs, outs = (y_pack, drows_pack), (y_theirs, drows_theirs), (y_any, drows_any)

    def to(j):
        return lax.rem(e + j, experts)

    def source(j):
        return lax.rem(e + experts - j, experts)

    def stage(k, slot):
        columns = pl.ds(pl.multiple_of(k * chunk, chunk), chunk)
        return (
            pltpu.make_async_copy(inner_any.at[0, :, columns], inner_stage.at[slot], stage_sem.at[0, slot]),
            pltpu.make_async_copy(outer_any.at[0, columns, :], outer_stage.at[slot], stage_sem.at[1, slot]),
        )

    def own_block(i):
        return pltpu.make_async_copy(ins[i].at[e], alls[i].at[a, e], own_sem.at[i])

    for slot in range(2):
        for copy in stage(slot, slot):
            copy.start()
    for i in range(2):
        own_block(i).start()
    greet([(a, to(j)) for j in range(1, experts)] + [across])

    def first_send(i, j):
        return remote(ins[i].at[to(j)], alls[i].at[a, e], in_send.at[i, j], in_recv.at[i, j], (a, to(j)))

    def forward_own(i):
        return remote(ins[i].at[e], alls[i].at[a, e], over_send.at[i, 0], over_recv.at[i, 0], across)

    def pass_on(i, j):
        block = alls[i].at[a, source(j)]
        return remote(block, block, over_send.at[i, j], over_recv.at[i, j], across)

    def received(i, j):
        block = alls[i].at[a, source(j)]
        return remote(block, block, in_send.at[i, j], in_recv.at[i, j], across)

    def from_across(i, j):
        block = alls[i].at[1 - a, source(j)]
        return remote(block, block, over_send.at[i, j], over_recv.at[i, j], across)

    def part_copy(i, j):
        return remote(
            packs[i].at[1 - a, to(j)], theirs[i].at[j], part_send.at[i, j], part_recv.at[i, j], across
        )

    def result_copy(i, j):
        return remote(packs[i].at[a, to(j)], outs[i].at[e], out_send.at[i, j], out_recv.at[i, j], (a, to(j)))

    for i in range(2):
        forward_own(i).start()

        @pl.loop(1, experts)
        def _(j):
            first_send(i, j).start()

    def take_in(i, k):
        @pl.when(k < steps - 1)
        def _():
            @pl.loop(0, each)
            def _(d):
                j = 1 + k * each + d

                @pl.when(j < experts)
                def _():
                    received(i, j).wait_recv()
                    pass_on(i, j).start()

    def hand_out(i, k):
        @pl.when(k < steps - 1)
        def _():
            @pl.loop(0, each)
            def _(d):
                j = 1 + k * each + d

                @pl.when(j < experts)
                def _():
                    part_copy(i, j).wait_recv()
                    at = to(j)
                    packs[i][a, at] = (packs[i][a, at].astype(full32) + theirs[i][j].astype(full32)).astype(low)
                    result_copy(i, j).start()

    @pl.loop(0, steps)
    def _(k):
        slot = lax.rem(k, 2)
        columns = pl.ds(pl.multiple_of(k * chunk, chunk), chunk)
        for copy in stage(k, slot):
            copy.wait()
        inner[:, columns] = inner_stage[slot].astype(low)
        outer[columns, :] = outer_stage[slot].astype(low)

        @pl.when(k + 2 < steps)
        def _():
            for copy in stage(k + 2, slot):
                copy.start()

        take_in(0, k)

    def unpack(i, place):
        own_block(i).wait()

        @pl.loop(0, experts)
        def _(j):
            from_across(i, j).wait_recv()

        group = 8
        for plane in range(dp):
            for s in range(0, experts, group):
                base = (plane * experts + s) * 8
                for b in range(full):
                    piece = alls[i][plane, s : s + group, :, b * width : (b + 1) * width].astype(full32)
                    place[pl.ds(b * count + base, 8 * group), :] = piece.reshape(8 * group, width).astype(low)
        tails = [
            alls[i][plane, :, :, full * width :].astype(full32).reshape(experts * 8, half) for plane in range(dp)
        ]
        tail = jnp.concatenate(tails, axis=0).astype(low)
        for right in range(2):
            place[pl.ds(full * count, count // 2), pl.ds(right * half, half)] = nn(
                tail_picks(count, right), tail
            ).astype(low)

    def pack(i):
        group = 8
        for plane in range(dp):
            for s in range(0, experts, group):
                base = (plane * experts + s) * 8
                for b in range(full):
                    piece = acc[pl.ds(b * count + base, 8 * group), :].reshape(group, 8, width)
                    packs[i][plane, s : s + group, :, b * width : (b + 1) * width] = piece.astype(low)
        tail = acc[pl.ds(full * count, count // 2), :].astype(low)
        spread = None
        for right in range(2):
            piece = lax.dot_general(
                tail_picks(count, right),
                tail[:, right * half : (right + 1) * half],
                (((0,), (0,)), ((), ())),
                preferred_element_type=full32,
            )
            spread = piece if spread is None else spread + piece
        for plane in range(dp):
            piece = spread[plane * experts * 8 : (plane + 1) * experts * 8].reshape(experts, 8, half)
            packs[i][plane, :, :, full * width :] = piece.astype(low)

        @pl.loop(0, experts)
        def _(d):
            part_copy(i, lax.rem(d + 1, experts)).start()

    unpack(0, rows)
    turned[...] = jnp.transpose(rows[...])
    acc[...] = jnp.zeros_like(acc)

    @pl.loop(0, steps)
    def _(k):
        columns = pl.ds(pl.multiple_of(k * chunk, chunk), chunk)
        z = nn(rows[...], inner[:, columns]) + hidden_ref[:, columns].astype(low).astype(full32)
        value, slope = gelu_both(z)
        act[:, columns] = value.astype(low)
        grad[:, columns] = slope
        acc[...] += nn(act[:, columns], outer[columns, :])
        take_in(1, k)

    part = return_ref.shape[1]
    bias = return_ref[...].astype(low).astype(full32)
    for i in range(dp):
        columns = pl.ds(i * part, part)
        acc[:, columns] = acc[:, columns] + jnp.where(a == i, bias, 0.0)
    pack(0)
    unpack(1, dy)
    total = jnp.zeros((1, width), full32)
    for i in range(rows.shape[0] // LANES):
        total = total + jnp.sum(dy[pl.ds(i * LANES, LANES), :].astype(full32), axis=0, keepdims=True)
    picked = total[:, :part]
    for i in range(1, dp):
        picked = jnp.where(a == i, total[:, i * part : (i + 1) * part], picked)
    dreturn_ref[...] = picked
    square[...] = jnp.zeros_like(square)
    flat = picked * picked
    for i in range(part // LANES):
        square[0:1, :] = square[0:1, :] + flat[:, i * LANES : (i + 1) * LANES]
    acc[...] = jnp.zeros_like(acc)

    @pl.loop(0, steps)
    def _(k):
        columns = pl.ds(pl.multiple_of(k * chunk, chunk), chunk)
        dz[:, columns] = (nt(dy[...], outer[columns, :]) * grad[:, columns]).astype(low)
        acc[...] += nt(dz[:, columns], inner[:, columns])
        hand_out(0, k)

    pack(1)

    def finish(i):
        part_copy(i, 0).wait_recv()
        packs[i][a, e] = (packs[i][a, e].astype(full32) + theirs[i][0].astype(full32)).astype(low)
        pltpu.make_async_copy(packs[i].at[a, e], outs[i].at[e], own_sem.at[i]).start()

    def store(k, slot):
        columns = pl.ds(pl.multiple_of(k * chunk, chunk), chunk)
        return (
            pltpu.make_async_copy(dinner_stage.at[slot], dinner_any.at[0, :, columns], store_sem.at[0, slot]),
            pltpu.make_async_copy(douter_stage.at[slot], douter_any.at[0, columns, :], store_sem.at[1, slot]),
        )

    finish(0)

    @pl.loop(0, steps)
    def _(k):
        slot = lax.rem(k, 2)
        columns = pl.ds(pl.multiple_of(k * chunk, chunk), chunk)
        douter = nn(jnp.transpose(act[:, columns]), dy[...])
        dinner = nn(turned[...], dz[:, columns])
        dhidden = jnp.sum(dz[:, columns].astype(full32), axis=0, keepdims=True)

        @pl.when(k >= 2)
        def _():
            for copy in store(k - 2, slot):
                copy.wait()

        douter_stage[slot] = douter.astype(low)
        dinner_stage[slot] = dinner.astype(low)
        for copy in store(k, slot):
            copy.start()
        dhidden_ref[:, columns] = dhidden
        parts = jnp.zeros((8, LANES), full32)
        folded = jnp.sum((douter * douter).reshape(-1, 8, width), axis=0)
        for i in range(width // LANES):
            parts = parts + folded[:, i * LANES : (i + 1) * LANES]
        folded = jnp.sum((dinner * dinner).reshape(-1, 8, chunk), axis=0)
        hidden_square = dhidden * dhidden
        for i in range(chunk // LANES):
            parts = parts + folded[:, i * LANES : (i + 1) * LANES]
            square[0:1, :] = square[0:1, :] + hidden_square[:, i * LANES : (i + 1) * LANES]
        square[...] += parts
        hand_out(1, k)

    finish(1)
    square_ref[...] = square[...]
    for k in range(steps - 2, steps):
        for copy in store(k, k % 2):
            copy.wait()
    for i in range(2):

        @pl.loop(1, experts)
        def _(j):
            block = outs[i].at[source(j)]
            remote(block, block, out_send.at[i, j], out_recv.at[i, j], across).wait_recv()

    for i in range(2):
        pltpu.make_async_copy(packs[i].at[a, e], outs[i].at[e], own_sem.at[i]).wait()
        forward_own(i).wait_send()
        part_copy(i, 0).wait_send()

        @pl.loop(1, experts)
        def _(j):
            first_send(i, j).wait_send()
            pass_on(i, j).wait_send()
            part_copy(i, j).wait_send()
            result_copy(i, j).wait_send()


def mixture(rows, dy, inner, hidden, outer, back, dp, cid, chunk=256):
    experts, _, packed = rows.shape
    width, units = inner.shape[1:]
    count = dp * experts * 8
    total = count * packed // width
    low, full = jnp.bfloat16, jnp.float32
    both = (dp, experts, 8, packed)
    sems = [pltpu.SemaphoreType.DMA((2, experts)) for _ in range(8)]
    return pl.pallas_call(
        functools.partial(moe_kernel, dp, experts, chunk),
        out_shape=[
            jax.ShapeDtypeStruct(rows.shape, low),
            jax.ShapeDtypeStruct(rows.shape, low),
            jax.ShapeDtypeStruct(inner.shape, low),
            jax.ShapeDtypeStruct(hidden.shape, full),
            jax.ShapeDtypeStruct(outer.shape, low),
            jax.ShapeDtypeStruct(back.shape, full),
            jax.ShapeDtypeStruct((8, LANES), full),
        ],
        in_specs=[ANY, ANY, ANY, VMEM, ANY, VMEM],
        out_specs=[ANY, ANY, ANY, VMEM, ANY, VMEM, VMEM],
        scratch_shapes=[
            pltpu.VMEM(both, low),
            pltpu.VMEM(both, low),
            pltpu.VMEM(both, low),
            pltpu.VMEM(both, low),
            pltpu.VMEM(both[1:], low),
            pltpu.VMEM(both[1:], low),
            pltpu.VMEM((total, width), low),
            pltpu.VMEM((width, total), low),
            pltpu.VMEM((total, width), low),
            pltpu.VMEM((width, units), low),
            pltpu.VMEM((units, width), low),
            pltpu.VMEM((total, units), low),
            pltpu.VMEM((total, units), full),
            pltpu.VMEM((total, units), low),
            pltpu.VMEM((total, width), full),
            pltpu.VMEM((2, width, chunk), full),
            pltpu.VMEM((2, chunk, width), full),
            pltpu.VMEM((2, width, chunk), low),
            pltpu.VMEM((2, chunk, width), low),
            pltpu.VMEM((8, LANES), full),
            pltpu.SemaphoreType.DMA((2,)),
            *sems,
            pltpu.SemaphoreType.DMA((2, 2)),
            pltpu.SemaphoreType.DMA((2, 2)),
        ],
        compiler_params=pltpu.CompilerParams(
            collective_id=cid, has_side_effects=True, vmem_limit_bytes=60 * 1024 * 1024
        ),
        cost_estimate=pl.CostEstimate(flops=17 * 10**9, bytes_accessed=25 * 10**6, transcendentals=2 * 10**6),
        name="mixture",
    )(rows, dy, inner, hidden, outer, back)


def adam_kernel(rates, decays, big, norm_ref, *refs):
    count = len(rates)
    ins, outs = refs[: 4 * count], refs[4 * count :]
    total = jnp.sum(jnp.sum(norm_ref[...], axis=0, keepdims=True), axis=1, keepdims=True)
    clip = THRESHOLD / jnp.maximum(jnp.sqrt(total), THRESHOLD)

    def update(i):
        weight, first, second, grad = ins[4 * i : 4 * i + 4]
        new = adam_update(
            weight[...],
            first[...],
            second[...],
            grad[...].astype(jnp.float32),
            clip,
            rates[i],
            decays[i],
        )
        for place, value in zip(outs[3 * i : 3 * i + 3], new):
            place[...] = value

    for i in range(big):
        update(i)

    @pl.when(pl.program_id(0) == 0)
    def _():
        for i in range(big, count):
            update(i)


def adam_all(squares, large, small, steps=8):
    groups = list(large) + list(small)
    specs, shapes, operands = [], [], []
    in_specs = [pl.BlockSpec(squares.shape, lambda i: (0, 0))]
    for g, group in enumerate(groups):
        shape = group[0].shape
        if g < len(large):
            spec = pl.BlockSpec((shape[0] // steps, shape[1]), lambda i: (i, 0))
        else:
            spec = pl.BlockSpec(shape, lambda i: (0, 0))
        in_specs += [spec] * 4
        specs += [spec] * 3
        shapes += [jax.ShapeDtypeStruct(shape, jnp.float32)] * 3
        operands += list(group[:4])
    rates, decays = [g[4] for g in groups], [g[5] for g in groups]
    out = pl.pallas_call(
        functools.partial(adam_kernel, rates, decays, len(large)),
        grid=(steps,),
        out_shape=shapes,
        in_specs=in_specs,
        out_specs=specs,
        compiler_params=pltpu.CompilerParams(
            vmem_limit_bytes=48 * 1024 * 1024, dimension_semantics=("arbitrary",)
        ),
        cost_estimate=pl.CostEstimate(flops=5 * 10**7, bytes_accessed=62 * 10**6, transcendentals=10**7),
        name="adam_all",
    )(squares, *operands)
    return [tuple(out[3 * i : 3 * i + 3]) for i in range(len(groups))]


def fits(dp, experts):
    return dp == 2 and experts == 16


def fast_shards(
    dp,
    experts,
    tokens,
    cotangent,
    expert_choice,
    priority,
    projection,
    projection_first,
    projection_second,
    output_weight,
    output_first,
    output_second,
    router_weight,
    router_first,
    router_second,
    vectors,
    vectors_first,
    vectors_second,
    expert_inner,
    inner_first,
    inner_second,
    hidden_bias,
    hidden_first,
    hidden_second,
    expert_outer,
    outer_first,
    outer_second,
    return_bias,
    return_first,
    return_second,
):
    model_width = tokens.shape[2]
    patches = tokens.shape[1]
    capacity = max(2, patches // experts)
    low = jnp.bfloat16
    shard_rows = projection.shape[0]
    wide = 3 * model_width
    used = wide + model_width + experts + vectors.shape[0]
    packed = jnp.concatenate(
        [projection, output_weight, router_weight, vectors.T, jnp.zeros((shard_rows, -used % 128), jnp.float32)], axis=1
    ).astype(low)
    weights = gather_blocks(packed, dp, experts, 1).reshape(model_width, packed.shape[1])
    rows, dy, qkv, ctx, mid, second, stat, aux, probs = forward(
        tokens[0], cotangent[0], expert_choice[0], priority[0], weights, experts, capacity
    )
    blocks = (experts, 8, rows.shape[1])
    returned, back_rows, inner_grad, hidden_grad, outer_grad, return_grad, expert_square = mixture(
        rows.reshape(blocks),
        dy.reshape(blocks),
        expert_inner,
        hidden_bias,
        expert_outer,
        return_bias,
        dp,
        2,
    )
    block_output, input_grad, local_grads = backward(
        tokens[0],
        cotangent[0],
        expert_choice[0],
        returned.reshape(rows.shape),
        back_rows.reshape(rows.shape),
        aux,
        probs,
        mid,
        second,
        ctx,
        stat,
        qkv,
        weights,
        experts,
        capacity,
    )
    chips = dp * experts // 2
    dense, squares = reduce_blocks(
        local_grads.reshape(chips, 2 * shard_rows, -1), expert_square, dp, experts, 4
    )
    cut = wide + model_width
    inner_new, outer_new, projection_new, output_new, router_new, vectors_new, hidden_new, return_new = adam_all(
        squares,
        [
            (expert_inner[0], inner_first[0], inner_second[0], inner_grad[0], RATE_INNER, DECAY),
            (expert_outer[0], outer_first[0], outer_second[0], outer_grad[0], RATE_OUTER, DECAY),
        ],
        [
            (projection, projection_first, projection_second, dense[:, :wide], RATE_PROJECTION, DECAY),
            (output_weight, output_first, output_second, dense[:, wide:cut], RATE_OUTPUT, DECAY),
            (router_weight, router_first, router_second, dense[:, cut : cut + experts], RATE_ROUTER, DECAY),
            (vectors, vectors_first, vectors_second, dense[:, cut + experts : used].T, RATE_VECTORS, 0.0),
            (hidden_bias, hidden_first, hidden_second, hidden_grad, RATE_HIDDEN, 0.0),
            (return_bias, return_first, return_second, return_grad, RATE_RETURN, 0.0),
        ],
    )
    return (
        block_output[None],
        input_grad[None],
        jnp.sqrt(jnp.sum(squares)),
        *projection_new,
        *output_new,
        *router_new,
        *vectors_new,
        *(v[None] for v in inner_new),
        *hidden_new,
        *(v[None] for v in outer_new),
        *return_new,
    )


def solution(mesh):
    dp, experts = mesh.shape["dp"], mesh.shape["expert"]
    body = functools.partial(fast_shards, dp, experts) if fits(dp, experts) else shards
    return jax.shard_map(
        body,
        mesh=mesh,
        in_specs=(
            P(("dp", "expert"), None, None),
            P(("dp", "expert"), None, None),
            P(("dp", "expert"), None, None),
            P(("dp", "expert"), None),
            P(("dp", "expert"), None),
            P(("dp", "expert"), None),
            P(("dp", "expert"), None),
            P(("dp", "expert"), None),
            P(("dp", "expert"), None),
            P(("dp", "expert"), None),
            P(("dp", "expert"), None),
            P(("dp", "expert"), None),
            P(("dp", "expert"), None),
            P(None, ("dp", "expert")),
            P(None, ("dp", "expert")),
            P(None, ("dp", "expert")),
            P("expert", None, "dp"),
            P("expert", None, "dp"),
            P("expert", None, "dp"),
            P("expert", "dp"),
            P("expert", "dp"),
            P("expert", "dp"),
            P("expert", "dp", None),
            P("expert", "dp", None),
            P("expert", "dp", None),
            P("expert", "dp"),
            P("expert", "dp"),
            P("expert", "dp"),
        ),
        out_specs=(
            P(("dp", "expert"), None, None),
            P(("dp", "expert"), None, None),
            P(),
            P(("dp", "expert"), None),
            P(("dp", "expert"), None),
            P(("dp", "expert"), None),
            P(("dp", "expert"), None),
            P(("dp", "expert"), None),
            P(("dp", "expert"), None),
            P(("dp", "expert"), None),
            P(("dp", "expert"), None),
            P(("dp", "expert"), None),
            P(None, ("dp", "expert")),
            P(None, ("dp", "expert")),
            P(None, ("dp", "expert")),
            P("expert", None, "dp"),
            P("expert", None, "dp"),
            P("expert", None, "dp"),
            P("expert", "dp"),
            P("expert", "dp"),
            P("expert", "dp"),
            P("expert", "dp", None),
            P("expert", "dp", None),
            P("expert", "dp", None),
            P("expert", "dp"),
            P("expert", "dp"),
            P("expert", "dp"),
        ),
        check_vma=False,
    )
```

profile of v0, /device:TPU:0, one launch (start us, length us, event | category | flops | bytes accessed | tf_op | source)
XLA Modules:
  0.0 309.7 jit_solution(7614494596757751124)
XLA Ops:
  0.7 0.0 copy-start.22
  0.7 1.0 convert.15
  1.7 0.9 convert.16
  2.5 0.7 convert.17
  3.2 0.1 copy.78
  3.3 0.7 convert.18
  4.0 0.1 copy.77
  4.1 0.8 concatenate.4.in_ref
  4.9 33.7 %gather_dense.1 = bf16[32,24,3200]{2,1,0:T(8,128)(2,1)} custom-call(bf16[24,3200]{1,0:T(8,128)(2,1)} %concatenate.4.in_ref), custom_call_target="tpu_custom_call" | custom-call | tf_op jit(solution)/shard_map/gather_dense/pallas_call | solution.py:563
  38.6 0.9 copy.76
  39.5 0.9 copy.79.rank_col
  40.4 27.6 %attend_forward.1 = (bf16[128,3456]{1,0:T(8,128)(2,1)}, bf16[128,3456]{1,0:T(8,128)(2,1)}, bf16[576,2304]{1,0:T(8,128)(2,1)}, bf16[576,768]{1,0:T(8,128)(2,1)}, ...) custom-call(bf16[576,768]{1,0:T(8,128)(2,1)} %bitcast.50, ...), custom_call_target="tpu_custom_call" | custom-call | flops 6000000000 | bytes 20000000 | tf_op jit(solution)/shard_map/attend_forward/pallas_call | solution.py:883
  68.0 109.4 %mixture.1 = (bf16[16,8,3456]{2,1,0:T(8,128)(2,1)}, bf16[16,8,3456]{2,1,0:T(8,128)(2,1)}, bf16[1,768,1536]{2,1,0:T(8,128)(2,1)}, f32[1,1536]{1,0:T(1,128)}, bf16...) custom-call(bf16[16,8,3456]{2,1,0:T(8,128)(2,1)} %bitcast.58, bf16[16,8,3456]{2,1,0:T(8,128)(2,1)} %bitcast.59, ...), custom_call_target="tpu_custom_call" | custom-call | flops 16999999488 | bytes 25000000 | tf_op jit(solution)/shard_map/mixture/pallas_call | solution.py:1473
  177.4 0.0 copy-start.3
  177.4 0.0 copy-start.4
  177.4 0.0 copy-start.5
  177.4 0.0 copy-start.10
  177.4 0.0 copy-start.11
  177.4 0.0 copy-start.12
  177.5 0.0 copy-start.13
  177.5 0.0 copy-start.14
  177.5 0.0 copy-start.15
  177.5 38.7 %attend_backward.1 = (bf16[576,768]{1,0:T(8,128)(2,1)}, f32[576,768]{1,0:T(8,128)}, bf16[768,3328]{1,0:T(8,128)(2,1)}) custom-call(bf16[576,768]{1,0:T(8,128)(2,1)} %bitcast.51, bf16[576,768]{1,0:T(8,128)(2,1)} %bitcast.53, s32[576,2]{1,0:T(8,128)} %bitcast.41, bf16[128,3456]{1,0:T(8,128)(2,1)} %bitcast.56, bf16[128,3456]{1,0:T(8,128)(2,1)} %bitcast.57, ...), custom_call_target="tpu_custom_call" | custom-call | flops 15000000512 | bytes 30000000 | tf_op jit(solution)/shard_map/attend_backward/pallas_call | solution.py:1115
  216.2 0.0 copy-start.9
  216.2 0.0 copy-done.16
  216.2 0.0 copy-start
  216.2 2.4 copy-done
  218.6 48.2 %reduce_dense.1 = (f32[24,3328]{1,0:T(8,128)S(1)}, f32[8,128]{1,0:T(8,128)S(1)}) custom-call(bf16[16,48,3328]{2,1,0:T(8,128)(2,1)S(1)} %bitcast.29, f32[8,128]{1,0:T(8,128)S(1)} %copy-done.16), custom_call_target="tpu_custom_call" | custom-call | tf_op jit(solution)/shard_map/reduce_dense/pallas_call | solution.py:671
  266.8 1.7 copy.80
  268.5 0.7 slice_bitcast_fusion.refs_23_
  269.2 0.8 copy.81.refs_16_
  270.0 0.8 copy.82.refs_17_
  270.8 0.8 copy.83.refs_18_
  271.5 0.0 copy-done.3
  271.6 0.0 copy-done.5
  271.6 1.7 copy-done.2
  273.3 0.9 copy-done.6
  274.2 0.9 copy-done.7
  275.1 0.9 copy-done.8
  276.0 0.7 copy-done.17
  276.7 0.7 copy-done.18
  277.4 0.7 copy-done.19
  278.1 0.7 copy-done.20
  278.7 26.1 %adam_all.1 = (f32[768,1536]{1,0:T(8,128)}, f32[768,1536]{1,0:T(8,128)}, f32[768,1536]{1,0:T(8,128)}, f32[1536,768]{1,0:T(8,128)}, f32[1536,768]{1,0:T(8,128)}, ...) custom-call(f32[8,128]{1,0:T(8,128)S(1)} %get-tuple-element.87.norm_, ...), custom_call_target="tpu_custom_call" | custom-call | flops 50000000 | bytes 62000000 | tf_op jit(solution)/shard_map/adam_all/pallas_call | solution.py:1564
  304.8 0.7 copy.84
  305.5 0.7 copy.85
  306.1 0.7 copy.86
  306.8 0.6 reduce_sum.9
  (26 shorter events, 0.1 us)
Async XLA Ops:
  0.7 37.9 %copy-start.21 = (s32[1,576,2]{1,2,0:T(2,128)S(1)}, s32[1,576,2]{1,2,0:T(2,128)}, u32[]{:S(2)}) copy-start(s32[1,576,2]{1,2,0:T(2,128)} %param.30) | copy-start | bytes 13828
  0.7 38.8 %copy-start.22 = (s32[1,576]{1,0:T(1,128)S(1)}, s32[1,576]{1,0:T(1,128)}, u32[]{:S(2)}) copy-start(s32[1,576]{1,0:T(1,128)} %rank_row.1) | copy-start | bytes 6916
  177.4 38.8 %copy-start.16 = (f32[8,128]{1,0:T(8,128)S(1)}, f32[8,128]{1,0:T(8,128)}, u32[]{:S(2)}) copy-start(f32[8,128]{1,0:T(8,128)} %get-tuple-element.86.part_ref) | copy-start | bytes 12292
  177.4 94.2 %copy-start.1 = (bf16[1,768,1536]{2,1,0:T(8,128)(2,1)S(1)}, bf16[1,768,1536]{2,1,0:T(8,128)(2,1)}, u32[]{:S(2)}) copy-start(bf16[1,768,1536]{2,1,0:T(8,128)(2,1)} %get-tuple-element.88) | copy-start | bytes 7077892
  177.4 94.2 %copy-start.3 = (f32[24,2304]{1,0:T(8,128)S(1)}, f32[24,2304]{1,0:T(8,128)}, u32[]{:S(2)}) copy-start(f32[24,2304]{1,0:T(8,128)} %refs_8_.1) | copy-start | bytes 663556
  177.4 94.2 %copy-start.4 = (f32[24,768]{1,0:T(8,128)S(1)}, f32[24,768]{1,0:T(8,128)}, u32[]{:S(2)}) copy-start(f32[24,768]{1,0:T(8,128)} %refs_12_.1) | copy-start | bytes 221188
  177.4 94.2 %copy-start.5 = (f32[24,2304]{1,0:T(8,128)S(1)}, f32[24,2304]{1,0:T(8,128)}, u32[]{:S(2)}) copy-start(f32[24,2304]{1,0:T(8,128)} %refs_9_.1) | copy-start | bytes 663556
  177.4 94.2 %copy-start.10 = (f32[1,1536]{1,0:T(1,128)S(1)}, f32[1,1536]{1,0:T(1,128)}, u32[]{:S(2)}) copy-start(f32[1,1536]{1,0:T(1,128)} %refs_24_.1) | copy-start | bytes 18436
  177.4 94.1 %copy-start.11 = (f32[1,1536]{1,0:T(1,128)S(1)}, f32[1,1536]{1,0:T(1,128)}, u32[]{:S(2)}) copy-start(f32[1,1536]{1,0:T(1,128)} %refs_25_.1) | copy-start | bytes 18436
  177.4 94.1 %copy-start.12 = (f32[1,1536]{1,0:T(1,128)S(1)}, f32[1,1536]{1,0:T(1,128)}, u32[]{:S(2)}) copy-start(f32[1,1536]{1,0:T(1,128)} %refs_26_.1) | copy-start | bytes 18436
  177.5 94.1 %copy-start.13 = (f32[1,1536]{1,0:T(1,128)S(1)}, f32[1,1536]{1,0:T(1,128)}, u32[]{:S(2)}) copy-start(f32[1,1536]{1,0:T(1,128)} %get-tuple-element.91.refs_27_) | copy-start | bytes 18436
  177.5 94.1 %copy-start.14 = (f32[7,24]{1,0:T(8,128)S(1)}, f32[7,24]{1,0:T(8,128)}, u32[]{:S(2)}) copy-start(f32[7,24]{1,0:T(8,128)} %refs_21_.1) | copy-start | bytes 2020
  177.5 94.1 %copy-start.15 = (f32[7,24]{1,0:T(8,128)S(1)}, f32[7,24]{1,0:T(8,128)}, u32[]{:S(2)}) copy-start(f32[7,24]{1,0:T(8,128)} %refs_22_.1) | copy-start | bytes 2020
  216.2 55.5 %copy-start.9 = (f32[7,24]{1,0:T(8,128)S(1)}, f32[7,24]{1,0:T(8,128)}, u32[]{:S(2)}) copy-start(f32[7,24]{1,0:T(8,128)} %refs_20_.1) | copy-start | bytes 2020
  216.2 2.5 copy-start
  271.6 1.7 copy-start.2
  273.3 0.9 copy-start.6
  274.2 0.9 copy-start.7
  275.1 0.9 copy-start.8
  276.0 0.7 copy-start.17
  276.7 0.7 copy-start.18
  277.4 0.7 copy-start.19
  278.0 0.7 copy-start.20
where the time goes:
time: 314 us; the launch traced here: 310 us
  Pallas kernels  284 us (90%)
  local copies, waits for them, and re-layouts  19 us (6%)
  other arithmetic  3.84 us (1%)
  between operations  3.22 us (1%)
    pallas_call x1, Pallas kernels, mixture(): pl.pallas_call(functools.partial(moe_kernel, dp, experts, chunk), out_sha...  109 us
    pallas_call x1, Pallas kernels, reduce_blocks(): pl.pallas_call(functools.partial(reduce_kernel, dp, experts), out_shape=[...  48.2 us
    pallas_call x1, Pallas kernels, backward(): pl.pallas_call(functools.partial(backward_kernel, experts, capacity, chun...  38.7 us
    pallas_call x1, Pallas kernels, gather_blocks(): pl.pallas_call(functools.partial(gather_kernel, dp, experts), out_shape=j...  33.7 us
    pallas_call x1, Pallas kernels, forward(): pl.pallas_call(functools.partial(forward_kernel, experts, capacity, chunk...  27.6 us
    pallas_call x1, Pallas kernels, adam_all(): pl.pallas_call(functools.partial(adam_kernel, rates, decays, len(large)),...  26.1 us
    unnamed x53, local copies, waits for them, and re-layouts  14.8 us

commit v1 on v0

--- a/solution.py
+++ b/solution.py
@@ -577,126 +577,6 @@
     )(block)
 
 
-def reduce_kernel(dp, experts, grad_ref, part_ref, out_ref, total_ref, own, rc, r3, r2, rz, fin, row, tiles,
-                  load, csend, crecv, send, recv, fsend, frecv, nsend, nrecv):
-    p = Place(dp, experts)
-    zs = p.zs
-    c = p.core
-    n = 4 * zs
-    world = dp * experts
-    half = own.shape[2]
-    deep = own.shape[1] // 2
-    partner = (p.a, p.e + 1 - 2 * c)
-    second = p.device(c, 0, 1, 0)
-    third = p.device(c, 0, 0, 1)
-    me = p.flat((p.a, p.e))
-    everyone = []
-    for j in range(1, world):
-        other = lax.rem(me + j, world)
-        everyone.append((lax.div(other, experts), lax.rem(other, experts)))
-    mycols = pl.ds(pl.multiple_of(c * half, 128), half)
-    hiscols = pl.ds(pl.multiple_of((1 - c) * half, 128), half)
-    order = list(range(2 * zs, n)) + list(range(zs, 2 * zs)) + list(range(1, zs)) + [0]
-    loads = {}
-    for k in order:
-        loads[k] = pltpu.make_async_copy(grad_ref.at[p.chip(c, *split_index(k, zs)), :, mycols], own.at[k], load.at[k])
-        loads[k].start()
-    greet(everyone)
-    pending = []
-
-    def push(src, dst, ss, rs, dev):
-        cp = remote(src, dst, ss, rs, dev)
-        cp.start()
-        pending.append(cp)
-
-    for k in order:
-        push(grad_ref.at[p.chip(1 - c, *split_index(k, zs)), :, hiscols], rc.at[k], csend.at[k], crecv.at[k], partner)
-
-    def got(ref, sem):
-        remote(ref, ref, sem, sem, partner).wait_recv()
-
-    for k in order:
-        loads[k].wait()
-        got(rc.at[k], crecv.at[k])
-        total = own[k].astype(jnp.float32) + rc[k].astype(jnp.float32)
-        if k < 2 * zs:
-            got(r3.at[k], recv.at[2 * zs + k])
-            total = total + r3[k].astype(jnp.float32)
-        if k < zs:
-            got(r2.at[k], recv.at[zs + k])
-            total = total + r2[k].astype(jnp.float32)
-        if k >= 1:
-            own[k] = total.astype(own.dtype)
-        if k >= 2 * zs:
-            push(own.at[k], r3.at[k - 2 * zs], send.at[k], recv.at[k], third)
-        elif k >= zs:
-            push(own.at[k], r2.at[k - zs], send.at[k], recv.at[k], second)
-        elif k >= 1:
-            push(own.at[k], rz.at[k - 1], send.at[k], recv.at[k], p.device(c, k, 0, 0))
-        else:
-            for j in range(1, zs):
-                got(rz.at[j - 1], recv.at[j])
-                total = total + rz[j - 1].astype(jnp.float32)
-            fin[...] = total
-    his = pl.ds(pl.multiple_of((1 - c) * deep, 8), deep)
-    mine = pl.ds(pl.multiple_of(c * deep, 8), deep)
-    push(fin.at[his], row, fsend, frecv, partner)
-    square = part_ref[...]
-    for i in range(2 * deep // 8):
-        for j in range(half // 128):
-            v = fin[pl.ds(8 * i, 8), pl.ds(128 * j, 128)]
-            square = square + v * v
-    tiles[me] = square
-    for j in range(1, world):
-        push(tiles.at[me], tiles.at[me], nsend.at[j], nrecv.at[j], everyone[j - 1])
-    out_ref[:, mycols] = fin[mine, :]
-    got(row, frecv)
-    out_ref[:, hiscols] = row[...]
-    for j in range(1, world):
-        src = lax.rem(me + world - j, world)
-        got(tiles.at[src], nrecv.at[j])
-    total = tiles[0]
-    for j in range(1, world):
-        total = total + tiles[j]
-    total_ref[...] = total
-    for cp in pending:
-        cp.wait_send()
-
-
-def reduce_blocks(grads, part, dp, experts, cid):
-    n = dp * experts
-    chips, rows, cols = grads.shape
-    half = cols // 2
-    bf = jnp.bfloat16
-    return pl.pallas_call(
-        functools.partial(reduce_kernel, dp, experts),
-        out_shape=[jax.ShapeDtypeStruct((rows // 2, cols), jnp.float32), jax.ShapeDtypeStruct((8, 128), jnp.float32)],
-        in_specs=[ANY, VMEM],
-        out_specs=[VMEM, VMEM],
-        scratch_shapes=[
-            pltpu.VMEM((chips, rows, half), bf),
-            pltpu.VMEM((chips, rows, half), bf),
-            pltpu.VMEM((chips // 2, rows, half), bf),
-            pltpu.VMEM((chips // 4, rows, half), bf),
-            pltpu.VMEM((chips // 4 - 1, rows, half), bf),
-            pltpu.VMEM((rows, half), jnp.float32),
-            pltpu.VMEM((rows // 2, half), jnp.float32),
-            pltpu.VMEM((n, 8, 128), jnp.float32),
-            pltpu.SemaphoreType.DMA((chips,)),
-            pltpu.SemaphoreType.DMA((chips,)),
-            pltpu.SemaphoreType.DMA((chips,)),
-            pltpu.SemaphoreType.DMA((chips,)),
-            pltpu.SemaphoreType.DMA((chips,)),
-            pltpu.SemaphoreType.DMA,
-            pltpu.SemaphoreType.DMA,
-            pltpu.SemaphoreType.DMA((n,)),
-            pltpu.SemaphoreType.DMA((n,)),
-        ],
-        compiler_params=pltpu.CompilerParams(collective_id=cid, has_side_effects=True, vmem_limit_bytes=32 * 1024 * 1024),
-        name="reduce_dense",
-    )(grads, part)
-
-
 LANES = 128
 
 
@@ -775,20 +655,20 @@
         unit, _ = norm_parts(tok_ref[part, :].astype(jnp.float32))
         normed[part, :] = (unit * row(0) + row(1)).astype(low)
     third = 256
-    for base, bias in ((0, 2), (width, None), (2 * width, 3)):
-        for j in range(width // third):
-            columns = pl.ds(base + j * third, third)
-            product = nn(normed[...], weights[:, columns])
-            if bias is not None:
-                product = product + vec[experts + bias : experts + bias + 1, pl.ds(j * third, third)]
-            qkv_ref[:, columns] = product.astype(low)
     stat_ref[...] = jnp.zeros_like(stat_ref)
 
     @pl.loop(0, width // LANES)
     def _(pair):
         at = pl.multiple_of(pair * LANES, LANES)
-        keys = qkv_ref[:, pl.ds(pl.multiple_of(width + at, LANES), LANES)]
-        values = qkv_ref[:, pl.ds(pl.multiple_of(2 * width + at, LANES), LANES)]
+        trio = pl.multiple_of(3 * at, LANES)
+        product = nn(normed[...], weights[:, pl.ds(trio, 3 * LANES)])
+        query_bias = vec[experts + 2 : experts + 3, pl.ds(at, LANES)]
+        value_bias = vec[experts + 3 : experts + 4, pl.ds(at, LANES)]
+        qkv_ref[:, pl.ds(trio, LANES)] = (product[:, :LANES] + query_bias).astype(low)
+        keys = product[:, LANES : 2 * LANES].astype(low)
+        values = (product[:, 2 * LANES :] + value_bias).astype(low)
+        qkv_ref[:, pl.ds(pl.multiple_of(trio + LANES, LANES), LANES)] = keys
+        qkv_ref[:, pl.ds(pl.multiple_of(trio + 2 * LANES, LANES), LANES)] = values
         key_lanes = lane_ids(patches)
         values_two = [
             jnp.where(key_lanes < HEAD_DIM, values, (key_lanes == HEAD_DIM).astype(jnp.float32).astype(low)),
@@ -796,7 +676,7 @@
         ]
         for part in row_parts(patches, chunk):
             own = lane_ids(chunk)
-            queries = qkv_ref[part, pl.ds(at, LANES)] * jnp.asarray(HEAD_DIM**-0.5, low)
+            queries = qkv_ref[part, pl.ds(trio, LANES)] * jnp.asarray(HEAD_DIM**-0.5, low)
             outs = []
             stat = stat_ref[part, :]
             for head in range(2):
@@ -914,7 +794,106 @@
     return hit.astype(jnp.float32).astype(jnp.bfloat16)
 
 
+class Stages:
+    def __init__(self, place, refs):
+        (self.grads, self.other, self.give3, self.take3, self.give2, self.take2, self.givez, self.takez, self.total) = refs[:9]
+        (self.cs, self.cr, self.s3, self.r3, self.s2, self.r2, self.sz, self.rz) = refs[9:]
+        self.p, self.zs, self.core = place, place.zs, place.core
+        self.partner = (place.a, place.e + 1 - 2 * place.core)
+
+    def to_partner(self, c):
+        return remote(
+            self.grads.at[c, 1 - self.core], self.other.at[c], self.cs.at[c], self.cr.at[c], self.partner
+        )
+
+    def to_third(self, c):
+        return remote(
+            self.give3.at[c], self.take3.at[c], self.s3.at[c], self.r3.at[c], self.p.device(self.core, 0, 0, 1)
+        )
+
+    def to_second(self, c):
+        return remote(
+            self.give2.at[c], self.take2.at[c], self.s2.at[c], self.r2.at[c], self.p.device(self.core, 0, 1, 0)
+        )
+
+    def along(self, c, dz):
+        return remote(
+            self.givez.at[c, dz - 1],
+            self.takez.at[c, dz - 1],
+            self.sz.at[c, dz],
+            self.rz.at[c, dz],
+            self.p.device(self.core, dz, 0, 0),
+        )
+
+    def sum_of(self, c, k, *more):
+        at = self.p.chip(self.core, *split_index(k, self.zs))
+        total = self.grads[c, self.core, at].astype(jnp.float32) + self.other[c, at].astype(jnp.float32)
+        for ref in more:
+            total = total + ref[c, k].astype(jnp.float32)
+        return total
+
+    def step0(self, c):
+        self.to_partner(c).start()
+
+    def step1(self, c):
+        self.to_partner(c).wait_recv()
+        zs = self.zs
+        for k in range(2 * zs, 4 * zs):
+            self.give3[c, k - 2 * zs] = self.sum_of(c, k).astype(self.give3.dtype)
+        self.to_third(c).start()
+
+    def step2(self, c):
+        self.to_third(c).wait_recv()
+        zs = self.zs
+        for k in range(zs, 2 * zs):
+            self.give2[c, k - zs] = self.sum_of(c, k, self.take3).astype(self.give2.dtype)
+        self.to_second(c).start()
+
+    def step3(self, c):
+        self.to_second(c).wait_recv()
+        for dz in range(1, self.zs):
+            self.givez[c, dz - 1] = self.sum_of(c, dz, self.take3, self.take2).astype(self.givez.dtype)
+            self.along(c, dz).start()
+
+    def step4(self, c):
+        total = self.sum_of(c, 0, self.take3, self.take2)
+        for dz in range(1, self.zs):
+            self.along(c, dz).wait_recv()
+            total = total + self.takez[c, dz - 1].astype(jnp.float32)
+        self.total[c] = total
+
+    def finish(self, count):
+        for c in range(count):
+            self.to_partner(c).wait_send()
+            self.to_third(c).wait_send()
+            self.to_second(c).wait_send()
+            for dz in range(1, self.zs):
+                self.along(c, dz).wait_send()
+
+
+def stage_scratch(chunks, chips, rows, columns):
+    low = jnp.bfloat16
+    zs = chips // 4
+    shapes = [
+        (chunks, 2, chips, rows, columns),
+        (chunks, chips, rows, columns),
+        (chunks, 2 * zs, rows, columns),
+        (chunks, 2 * zs, rows, columns),
+        (chunks, zs, rows, columns),
+        (chunks, zs, rows, columns),
+        (chunks, zs - 1, rows, columns),
+        (chunks, zs - 1, rows, columns),
+    ]
+    sems = [pltpu.SemaphoreType.DMA((chunks,)) for _ in range(6)]
+    sems += [pltpu.SemaphoreType.DMA((chunks, zs)) for _ in range(2)]
+    return [pltpu.VMEM(s, low) for s in shapes] + [pltpu.VMEM((chunks, rows, columns), jnp.float32)] + sems
+
+
+STAGE_REFS = 17
+
+
 def backward_kernel(
+    dp,
     experts,
     capacity,
     chunk,
@@ -922,22 +901,29 @@
     cot_ref,
     choice_ref,
     ret_ref,
-    back_ref,
     aux_ref,
     probs_ref,
     mid_ref,
+    part_ref,
+    back_any,
+    second_any,
+    ctx_any,
+    stat_any,
+    qkv_any,
+    weights_any,
+    out_ref,
+    input_ref,
+    dense_ref,
+    total_ref,
+    back_ref,
     second_ref,
     ctx_ref,
     stat_ref,
     qkv_ref,
-    weights_any,
-    out_ref,
-    input_ref,
-    grad_ref,
     weights,
     vec,
     stacked,
-    normed,
+    normed_turned,
     branch,
     dctx,
     joined,
@@ -946,19 +932,52 @@
     work,
     sums,
     load,
+    row,
+    row_tail,
+    tiles,
+    row_send,
+    row_recv,
+    tile_send,
+    tile_recv,
+    *stage_refs,
 ):
-    low = jnp.bfloat16
+    low, full32 = jnp.bfloat16, jnp.float32
     patches, width = tok_ref.shape
-    fetch = pltpu.make_async_copy(weights_any, weights, load)
-    fetch.start()
+    trio_width = 3 * LANES
+    p = Place(dp, experts)
+    world = dp * experts
+    me = p.flat((p.a, p.e))
+    main, last = Stages(p, stage_refs[:STAGE_REFS]), Stages(p, stage_refs[STAGE_REFS:])
+    chips, shard2 = main.grads.shape[2:4]
+    pieces = [
+        (back_any, back_ref),
+        (weights_any, weights),
+        (ctx_any, ctx_ref),
+        (second_any, second_ref),
+        (stat_any, stat_ref),
+        (qkv_any, qkv_ref),
+    ]
+    fetch = [pltpu.make_async_copy(s, d, load.at[i]) for i, (s, d) in enumerate(pieces)]
+    for copy in fetch:
+        copy.start()
+    barrier = pltpu.get_barrier_semaphore()
+
+    def other_device(j):
+        at = lax.rem(me + j, world)
+        return lax.div(at, experts), lax.rem(at, experts)
+
+    @pl.loop(1, world)
+    def _(j):
+        pl.semaphore_signal(barrier, inc=1, device_id=other_device(j), device_id_type=MESH)
+
     full = capacity // 8
     half = width // 2
     lanes = lane_ids(patches)
     aux = aux_ref[...]
     slots = [aux[:, i : i + 1] for i in range(4)]
     gates = [aux[:, 4 + i : 5 + i] for i in range(2)]
-    ids = lax.broadcasted_iota(jnp.int32, (patches, full * LANES), 1).astype(jnp.float32)
-    tail_ids = lane_ids(patches, full * LANES).astype(jnp.float32)
+    ids = lax.broadcasted_iota(jnp.int32, (patches, full * LANES), 1).astype(full32)
+    tail_ids = lane_ids(patches, full * LANES).astype(full32)
     hits = [ids == slots[0], ids == slots[1]]
     lefts = [tail_ids == slots[0], tail_ids == slots[1]]
     rights = [tail_ids == slots[2], tail_ids == slots[3]]
@@ -967,7 +986,7 @@
         return (jnp.where(marks[0], gates[0], 0.0) + jnp.where(marks[1], gates[1], 0.0)).astype(low)
 
     def pick(marks):
-        return (marks[0] | marks[1]).astype(jnp.float32).astype(low)
+        return (marks[0] | marks[1]).astype(full32).astype(low)
 
     for i in range(full):
         stacked[pl.ds(i * LANES, LANES), :] = ret_ref[:, pl.ds(i * width, width)]
@@ -978,7 +997,7 @@
     out_ref[:, half:] = (mid_ref[:, half:] + (final[:, half:] + right_mix)).astype(low)
     along = nt(cot_ref[...], stacked[...])
     along_left, along_right = nt(cot_ref[:, :half], tail), nt(cot_ref[:, half:], tail)
-    dprobs = jnp.zeros((patches, LANES), jnp.float32)
+    dprobs = jnp.zeros((patches, LANES), full32)
     for j in range(2):
         dgate = jnp.sum(jnp.where(hits[j], along, 0.0), axis=1, keepdims=True) + jnp.sum(
             jnp.where(lefts[j], along_left, 0.0) + jnp.where(rights[j], along_right, 0.0), axis=1, keepdims=True
@@ -986,13 +1005,14 @@
         dprobs = dprobs + jnp.where(lanes == choice_ref[:, j : j + 1], dgate, 0.0)
     probs = probs_ref[...]
     dlogits = (probs * (dprobs - jnp.sum(probs * dprobs, axis=1, keepdims=True))).astype(low)
+    fetch[0].wait()
     for i in range(full):
         stacked[pl.ds(i * LANES, LANES), :] = back_ref[:, pl.ds(i * width, width)]
     tail = back_ref[:, pl.ds(full * width, half)]
-    fetch.wait()
+    fetch[1].wait()
     vec[...] = vector_table(weights, width)
 
-    def row(i):
+    def vector(i):
         return vec[experts + i : experts + i + 1, :]
 
     routed = weights[:, 4 * width :]
@@ -1019,39 +1039,47 @@
         grad = work[part, :]
         column_sum(5, grad * unit)
         column_sum(6, grad)
-        total = cot_ref[part, :].astype(jnp.float32) + norm_back(grad, unit, inverse, row(5))
+        total = cot_ref[part, :].astype(full32) + norm_back(grad, unit, inverse, vector(5))
         dmid[part, :] = total
         rounded = total.astype(low)
         branch[part, :] = rounded
-        column_sum(4, rounded.astype(jnp.float32))
+        column_sum(4, rounded.astype(full32))
+    fetch[2].wait()
+    ctx_turned = jnp.transpose(ctx_ref[...])
+    for core in range(2):
+        columns = pl.ds(core * half, half)
+        product = nn(ctx_turned, branch[:, columns])
+        main.grads[0, core] = product.reshape(chips, shard2, half).astype(low)
+    pl.semaphore_wait(barrier, world - 1)
+    main.step0(0)
     third = 256
     for j in range(width // third):
         rows = pl.ds(j * third, third)
         dctx[:, rows] = nt(branch[...], weights[rows, pl.ds(3 * width, width)]).astype(low)
-    second_turned = jnp.transpose(second_ref[...])
-    router_grad = nn(second_turned, dlogits)
-    ctx_turned = jnp.transpose(ctx_ref[...])
-    for j in range(width // third):
-        columns = pl.ds(j * third, third)
-        grad_ref[:, pl.ds(3 * width + j * third, third)] = nn(ctx_turned, branch[:, columns]).astype(low)
+    fetch[3].wait()
+    router_rows = nn(jnp.transpose(dlogits.astype(full32)).astype(low), second_ref[...])
+    for part in row_parts(patches, chunk):
+        unit, _ = norm_parts(tok_ref[part, :].astype(full32))
+        second_ref[part, :] = (unit * vector(0) + vector(1)).astype(low)
+    normed_turned[...] = jnp.transpose(second_ref[...])
     heads = (
         lax.broadcasted_iota(jnp.int32, (16, width), 1) // HEAD_DIM == lax.broadcasted_iota(jnp.int32, (16, width), 0)
-    ).astype(jnp.float32).astype(low)
-    product = dctx[...].astype(jnp.float32) * ctx_ref[...].astype(jnp.float32)
+    ).astype(full32).astype(low)
+    product = dctx[...].astype(full32) * ctx_ref[...].astype(full32)
     upper = product.astype(low)
-    center = nt(heads, upper) + nt(heads, (product - upper.astype(jnp.float32)).astype(low))
+    center = nt(heads, upper) + nt(heads, (product - upper.astype(full32)).astype(low))
+    fetch[4].wait()
     logs = jnp.transpose(stat_ref[...])
-    sums_rows = jnp.concatenate([logs[:16], center], axis=0)
-    vec_rows = work
-    vec_rows[0:32, :patches] = sums_rows
-
-    @pl.loop(0, width // LANES)
-    def _(pair):
+    work[0:32, :patches] = jnp.concatenate([logs[:16], center], axis=0)
+    fetch[5].wait()
+
+    def attend(pair, c, core):
         at = pl.multiple_of(pair * LANES, LANES)
-        key_at = pl.ds(pl.multiple_of(width + at, LANES), LANES)
-        value_at = pl.ds(pl.multiple_of(2 * width + at, LANES), LANES)
+        trio = pl.multiple_of(pair * trio_width, LANES)
+        key_at = pl.ds(pl.multiple_of(trio + LANES, LANES), LANES)
+        value_at = pl.ds(pl.multiple_of(trio + 2 * LANES, LANES), LANES)
         scale = jnp.asarray(HEAD_DIM**-0.5, low)
-        queries = qkv_ref[:, pl.ds(at, LANES)] * scale
+        queries = qkv_ref[:, pl.ds(trio, LANES)] * scale
         given = dctx[:, pl.ds(at, LANES)]
         own = lane_ids(patches)
         zero = jnp.zeros_like(queries)
@@ -1071,61 +1099,164 @@
                 value_out.append(nn(prob.astype(low), given))
                 dscore = (prob * (nt(values, head_given[head]) - center_row)).astype(low)
                 key_out.append(nn(dscore, queries))
-                piece = nn(turned_keys[HEAD_DIM * head : HEAD_DIM * (head + 1), part.start : part.start + part.size], dscore)
+                head_keys = turned_keys[HEAD_DIM * head : HEAD_DIM * (head + 1), part.start : part.start + part.size]
+                piece = nn(head_keys, dscore)
                 query_parts[head] = piece if query_parts[head] is None else query_parts[head] + piece
             side = lane_ids(chunk) < HEAD_DIM
             joined[part, key_at] = jnp.where(side, key_out[0], key_out[1]).astype(low)
             joined[part, value_at] = jnp.where(side, value_out[0], value_out[1]).astype(low)
         turned_query[...] = jnp.concatenate(query_parts, axis=0)
-        joined[:, pl.ds(at, LANES)] = jnp.transpose(turned_query[...]).astype(low)
-
-    for part in row_parts(patches, chunk):
-        unit, _ = norm_parts(tok_ref[part, :].astype(jnp.float32))
-        normed[part, :] = (unit * row(0) + row(1)).astype(low)
-        column_sum(2, joined[part, :width].astype(jnp.float32))
-        column_sum(3, joined[part, 2 * width :].astype(jnp.float32))
-    normed_turned = jnp.transpose(normed[...])
-    for j in range(3 * width // third):
-        columns = pl.ds(j * third, third)
-        grad_ref[:, columns] = nn(normed_turned, joined[:, columns]).astype(low)
+        joined[:, pl.ds(trio, LANES)] = jnp.transpose(turned_query[...]).astype(low)
+        product = nn(normed_turned[...], joined[:, pl.ds(trio, trio_width)])
+        main.grads[c, core] = product.reshape(chips, shard2, trio_width).astype(low)
+
+    pair_chunks = width // LANES // 2
+
+    for i in range(pair_chunks):
+        attend(2 * i, i + 1, 0)
+        main.step1(i)
+        if i >= 1:
+            main.step3(i - 1)
+        attend(2 * i + 1, i + 1, 1)
+        main.step0(i + 1)
+        main.step2(i)
+        if i >= 1:
+            main.step4(i - 1)
+
+    end = pair_chunks
+    ones = jnp.ones((8, patches), low)
+    for j in range(width // LANES):
+        column_parts = nn(ones, joined[:, pl.ds(j * trio_width, trio_width)])
+        sums[16:17, pl.ds(j * LANES, LANES)] = column_parts[0:1, :LANES]
+        sums[24:25, pl.ds(j * LANES, LANES)] = column_parts[0:1, 2 * LANES :]
     for j in range(width // third):
         rows = pl.ds(j * third, third)
         work[:, rows] = nt(joined[...], weights[rows, : 3 * width])
-    for part in row_parts(patches, chunk):
-        unit, inverse = norm_parts(tok_ref[part, :].astype(jnp.float32))
+        if j == 0:
+            main.step1(end)
+            main.step3(end - 1)
+    main.step2(end)
+    main.step4(end - 1)
+    parts = row_parts(patches, chunk)
+    for part in parts:
+        unit, inverse = norm_parts(tok_ref[part, :].astype(full32))
         grad = work[part, :]
         column_sum(0, grad * unit)
         column_sum(1, grad)
-        input_ref[part, :] = dmid[part, :] + norm_back(grad, unit, inverse, row(0))
-    vec[...] = jnp.zeros_like(vec)
+        input_ref[part, :] = dmid[part, :] + norm_back(grad, unit, inverse, vector(0))
+    vec[...] = router_rows
     for i in range(7):
         vec[experts + i : experts + i + 1, :] = jnp.sum(sums[pl.ds(8 * i, 8), :], axis=0, keepdims=True)
-    last = router_grad + jnp.transpose(vec[...])
-    grad_ref[:, pl.ds(4 * width, LANES)] = last.astype(low)
-    rest = grad_ref.shape[1] - 4 * width - LANES
-    grad_ref[:, pl.ds(4 * width + LANES, rest)] = jnp.zeros((width, rest), low)
+    last.grads[0, 0] = jnp.transpose(vec[...]).reshape(chips, shard2, LANES).astype(low)
+    last.grads[0, 1] = jnp.zeros((chips, shard2, LANES), low)
+    last.step0(0)
+    main.step3(end)
+    last.step1(0)
+    last.step2(0)
+    main.step4(end)
+    last.step3(0)
+    last.step4(0)
+    deep = shard2 // 2
+    his = pl.ds(pl.multiple_of((1 - p.core) * deep, 8), deep)
+    mine = pl.ds(pl.multiple_of(p.core * deep, 8), deep)
+    rows_copy = [
+        remote(main.total.at[:, his], row, row_send.at[0], row_recv.at[0], main.partner),
+        remote(last.total.at[:, his], row_tail, row_send.at[1], row_recv.at[1], main.partner),
+    ]
+    for copy in rows_copy:
+        copy.start()
+    square = part_ref[...]
+    for stage, count in ((main, end + 1), (last, 1)):
+        for c in range(count):
+            values = stage.total[c]
+            folded = jnp.sum((values * values).reshape(-1, 8, values.shape[1]), axis=0)
+            for j in range(values.shape[1] // LANES):
+                square = square + folded[:, j * LANES : (j + 1) * LANES]
+    tiles[me] = square
+
+    def tile_copy(j):
+        return remote(tiles.at[me], tiles.at[me], tile_send.at[j], tile_recv.at[j], other_device(j))
+
+    @pl.loop(1, world)
+    def _(j):
+        tile_copy(j).start()
+
+    def put(core, values, tail_values):
+        for c in range(end + 1):
+            dense_ref[:, pl.ds(pl.multiple_of(c * width + core * half, LANES), half)] = values(c)
+        dense_ref[:, pl.ds(pl.multiple_of(4 * width + core * LANES, LANES), LANES)] = tail_values
+
+    put(p.core, lambda c: main.total[c, mine, :], last.total[0, mine, :])
+    for copy in rows_copy:
+        copy.wait_recv()
+    put(1 - p.core, lambda c: row[c], row_tail[0])
+
+    @pl.loop(1, world)
+    def _(j):
+        block = tiles.at[lax.rem(me + world - j, world)]
+        remote(block, block, tile_send.at[j], tile_recv.at[j], main.partner).wait_recv()
+
+    total = tiles[0]
+    for j in range(1, world):
+        total = total + tiles[j]
+    total_ref[...] = total
+    main.finish(end + 1)
+    last.finish(1)
+    for copy in rows_copy:
+        copy.wait_send()
+
+    @pl.loop(1, world)
+    def _(j):
+        tile_copy(j).wait_send()
 
 
 def backward(
-    tokens, cotangent, choice, ret, back, aux, probs, mid, second, ctx, stat, qkv, weights, experts, capacity, chunk=192
+    tokens,
+    cotangent,
+    choice,
+    ret,
+    back,
+    aux,
+    probs,
+    mid,
+    second,
+    ctx,
+    stat,
+    qkv,
+    weights,
+    part,
+    dp,
+    experts,
+    capacity,
+    cid,
+    chunk=192,
 ):
     patches, width = tokens.shape
     low, full = jnp.bfloat16, jnp.float32
-    columns = -(-weights.shape[1] // 256) * 256
+    world = dp * experts
+    chips, rows = world // 2, 2 * width // world
+    chunks = width // LANES // 2 + 1
+    columns = 4 * width + 2 * LANES
     return pl.pallas_call(
-        functools.partial(backward_kernel, experts, capacity, chunk),
+        functools.partial(backward_kernel, dp, experts, capacity, chunk),
         out_shape=[
             jax.ShapeDtypeStruct((patches, width), low),
             jax.ShapeDtypeStruct((patches, width), full),
-            jax.ShapeDtypeStruct((width, columns), low),
+            jax.ShapeDtypeStruct((rows // 2, columns), full),
+            jax.ShapeDtypeStruct((8, LANES), full),
         ],
-        in_specs=[VMEM] * 12 + [ANY],
-        out_specs=[VMEM] * 3,
+        in_specs=[VMEM] * 8 + [ANY] * 6,
+        out_specs=[VMEM] * 4,
         scratch_shapes=[
+            pltpu.VMEM(back.shape, low),
+            pltpu.VMEM((patches, width), low),
+            pltpu.VMEM((patches, width), low),
+            pltpu.VMEM(stat.shape, full),
+            pltpu.VMEM(qkv.shape, low),
             pltpu.VMEM(weights.shape, low),
             pltpu.VMEM((LANES, width), full),
             pltpu.VMEM((capacity // 8 * LANES, width), low),
-            pltpu.VMEM((patches, width), low),
+            pltpu.VMEM((width, patches), low),
             pltpu.VMEM((patches, width), low),
             pltpu.VMEM((patches, width), low),
             pltpu.VMEM((patches, 3 * width), low),
@@ -1133,12 +1264,23 @@
             pltpu.VMEM((patches, width), full),
             pltpu.VMEM((patches, width), full),
             pltpu.VMEM((56, width), full),
-            pltpu.SemaphoreType.DMA,
+            pltpu.SemaphoreType.DMA((6,)),
+            pltpu.VMEM((chunks, rows // 2, width // 2), full),
+            pltpu.VMEM((1, rows // 2, LANES), full),
+            pltpu.VMEM((world, 8, LANES), full),
+            pltpu.SemaphoreType.DMA((2,)),
+            pltpu.SemaphoreType.DMA((2,)),
+            pltpu.SemaphoreType.DMA((world,)),
+            pltpu.SemaphoreType.DMA((world,)),
+            *stage_scratch(chunks, chips, rows, width // 2),
+            *stage_scratch(1, chips, rows, LANES),
         ],
-        compiler_params=pltpu.CompilerParams(vmem_limit_bytes=60 * 1024 * 1024),
+        compiler_params=pltpu.CompilerParams(
+            collective_id=cid, has_side_effects=True, vmem_limit_bytes=60 * 1024 * 1024
+        ),
         cost_estimate=pl.CostEstimate(flops=15 * 10**9, bytes_accessed=30 * 10**6, transcendentals=4 * 10**6),
         name="attend_backward",
-    )(tokens, cotangent, choice, ret, back, aux, probs, mid, second, ctx, stat, qkv, weights)
+    )(tokens, cotangent, choice, ret, aux, probs, mid, part, back, second, ctx, stat, qkv, weights)
 
 
 def moe_kernel(
@@ -1517,63 +1659,86 @@
     )(rows, dy, inner, hidden, outer, back)
 
 
-def adam_kernel(rates, decays, big, norm_ref, *refs):
-    count = len(rates)
-    ins, outs = refs[: 4 * count], refs[4 * count :]
+def adam_values(weight, first, second, gradient, clip, rate, decay):
+    scaled = gradient * clip
+    first_new = BETA_ONE * first + (1.0 - BETA_ONE) * scaled
+    second_new = BETA_TWO * second + (1.0 - BETA_TWO) * scaled * scaled
+    first_hat = first_new * (1.0 / (1.0 - BETA_ONE**STEP))
+    second_hat = second_new * (1.0 / (1.0 - BETA_TWO**STEP))
+    weight_new = weight - rate * (first_hat / (jnp.sqrt(second_hat) + ADAM_EPS) + decay * weight)
+    return weight_new, first_new, second_new
+
+
+def adam_kernel(experts, norm_ref, dense_ref, *refs):
+    ins, outs = refs[:28], refs[28:]
     total = jnp.sum(jnp.sum(norm_ref[...], axis=0, keepdims=True), axis=1, keepdims=True)
-    clip = THRESHOLD / jnp.maximum(jnp.sqrt(total), THRESHOLD)
-
-    def update(i):
-        weight, first, second, grad = ins[4 * i : 4 * i + 4]
-        new = adam_update(
-            weight[...],
-            first[...],
-            second[...],
-            grad[...].astype(jnp.float32),
-            clip,
-            rates[i],
-            decays[i],
-        )
+    norm = jnp.sqrt(total)
+    clip = THRESHOLD / jnp.maximum(norm, THRESHOLD)
+
+    def update(i, grad, rate, decay, columns=slice(None)):
+        weight, first, second = (ref[:, columns] for ref in ins[3 * i : 3 * i + 3])
+        new = adam_values(weight, first, second, grad, clip, rate, decay)
         for place, value in zip(outs[3 * i : 3 * i + 3], new):
-            place[...] = value
-
-    for i in range(big):
-        update(i)
+            place[:, columns] = value
+
+    inner_grad, outer_grad, hidden_grad, return_grad = ins[24:28]
+    update(0, inner_grad[...].astype(jnp.float32), RATE_INNER, DECAY)
+    update(1, outer_grad[...].astype(jnp.float32), RATE_OUTER, DECAY)
 
     @pl.when(pl.program_id(0) == 0)
     def _():
-        for i in range(big, count):
-            update(i)
-
-
-def adam_all(squares, large, small, steps=8):
-    groups = list(large) + list(small)
-    specs, shapes, operands = [], [], []
-    in_specs = [pl.BlockSpec(squares.shape, lambda i: (0, 0))]
-    for g, group in enumerate(groups):
-        shape = group[0].shape
-        if g < len(large):
-            spec = pl.BlockSpec((shape[0] // steps, shape[1]), lambda i: (i, 0))
-        else:
-            spec = pl.BlockSpec(shape, lambda i: (0, 0))
-        in_specs += [spec] * 4
-        specs += [spec] * 3
-        shapes += [jax.ShapeDtypeStruct(shape, jnp.float32)] * 3
-        operands += list(group[:4])
-    rates, decays = [g[4] for g in groups], [g[5] for g in groups]
+        outs[24][...] = norm
+        width = ins[9].shape[1]
+        trio = 3 * LANES
+        for pair in range(width // LANES):
+            for kind in range(3):
+                update(
+                    2,
+                    dense_ref[:, width + pair * trio + kind * LANES : width + pair * trio + (kind + 1) * LANES],
+                    RATE_PROJECTION,
+                    DECAY,
+                    slice(kind * width + pair * LANES, kind * width + (pair + 1) * LANES),
+                )
+        update(3, dense_ref[:, :width], RATE_OUTPUT, DECAY)
+        turned = jnp.transpose(dense_ref[:, 4 * width : 4 * width + LANES])
+        update(4, turned[:experts], RATE_ROUTER, DECAY)
+        update(5, turned[experts : experts + 7], RATE_VECTORS, 0.0)
+        update(6, hidden_grad[...], RATE_HIDDEN, 0.0)
+        update(7, return_grad[...], RATE_RETURN, 0.0)
+
+
+def adam_all(experts, squares, dense, states, grads, steps=8):
+    operands, in_specs, out_specs, shapes = [squares, dense], [], [], []
+
+    def spec_of(array, blocks):
+        shape = array.shape
+        if blocks:
+            return pl.BlockSpec((shape[0] // steps, shape[1]), lambda i: (i, 0))
+        return pl.BlockSpec(shape, lambda i: (0, 0))
+
+    in_specs += [spec_of(squares, False), spec_of(dense, False)]
+    for g, group in enumerate(states):
+        spec = spec_of(group[0], g < 2)
+        in_specs += [spec] * 3
+        out_specs += [spec] * 3
+        shapes += [jax.ShapeDtypeStruct(group[0].shape, jnp.float32)] * 3
+        operands += list(group)
+    for g, grad in enumerate(grads):
+        in_specs.append(spec_of(grad, g < 2))
+        operands.append(grad)
     out = pl.pallas_call(
-        functools.partial(adam_kernel, rates, decays, len(large)),
+        functools.partial(adam_kernel, experts),
         grid=(steps,),
-        out_shape=shapes,
+        out_shape=shapes + [jax.ShapeDtypeStruct((1, 1), jnp.float32)],
         in_specs=in_specs,
-        out_specs=specs,
+        out_specs=out_specs + [pl.BlockSpec((1, 1), lambda i: (0, 0))],
         compiler_params=pltpu.CompilerParams(
-            vmem_limit_bytes=48 * 1024 * 1024, dimension_semantics=("arbitrary",)
+            vmem_limit_bytes=60 * 1024 * 1024, dimension_semantics=("arbitrary",)
         ),
         cost_estimate=pl.CostEstimate(flops=5 * 10**7, bytes_accessed=62 * 10**6, transcendentals=10**7),
         name="adam_all",
-    )(squares, *operands)
-    return [tuple(out[3 * i : 3 * i + 3]) for i in range(len(groups))]
+    )(*operands)
+    return [tuple(out[3 * i : 3 * i + 3]) for i in range(len(states))], out[-1].reshape(())
 
 
 def fits(dp, experts):
@@ -1617,10 +1782,10 @@
     capacity = max(2, patches // experts)
     low = jnp.bfloat16
     shard_rows = projection.shape[0]
-    wide = 3 * model_width
-    used = wide + model_width + experts + vectors.shape[0]
+    used = 4 * model_width + experts + vectors.shape[0]
+    by_pair = projection.reshape(shard_rows, 3, -1, LANES).transpose(0, 2, 1, 3).reshape(projection.shape)
     packed = jnp.concatenate(
-        [projection, output_weight, router_weight, vectors.T, jnp.zeros((shard_rows, -used % 128), jnp.float32)], axis=1
+        [by_pair, output_weight, router_weight, vectors.T, jnp.zeros((shard_rows, -used % 128), jnp.float32)], axis=1
     ).astype(low)
     weights = gather_blocks(packed, dp, experts, 1).reshape(model_width, packed.shape[1])
     rows, dy, qkv, ctx, mid, second, stat, aux, probs = forward(
@@ -1637,7 +1802,7 @@
         dp,
         2,
     )
-    block_output, input_grad, local_grads = backward(
+    block_output, input_grad, dense, squares = backward(
         tokens[0],
         cotangent[0],
         expert_choice[0],
@@ -1651,36 +1816,36 @@
         stat,
         qkv,
         weights,
+        expert_square,
+        dp,
         experts,
         capacity,
-    )
-    chips = dp * experts // 2
-    dense, squares = reduce_blocks(
-        local_grads.reshape(chips, 2 * shard_rows, -1), expert_square, dp, experts, 4
-    )
-    cut = wide + model_width
-    inner_new, outer_new, projection_new, output_new, router_new, vectors_new, hidden_new, return_new = adam_all(
+        4,
+    )
+    states, grad_norm = adam_all(
+        experts,
         squares,
+        dense,
         [
-            (expert_inner[0], inner_first[0], inner_second[0], inner_grad[0], RATE_INNER, DECAY),
-            (expert_outer[0], outer_first[0], outer_second[0], outer_grad[0], RATE_OUTER, DECAY),
+            (expert_inner[0], inner_first[0], inner_second[0]),
+            (expert_outer[0], outer_first[0], outer_second[0]),
+            (projection, projection_first, projection_second),
+            (output_weight, output_first, output_second),
+            (router_weight.T, router_first.T, router_second.T),
+            (vectors, vectors_first, vectors_second),
+            (hidden_bias, hidden_first, hidden_second),
+            (return_bias, return_first, return_second),
         ],
-        [
-            (projection, projection_first, projection_second, dense[:, :wide], RATE_PROJECTION, DECAY),
-            (output_weight, output_first, output_second, dense[:, wide:cut], RATE_OUTPUT, DECAY),
-            (router_weight, router_first, router_second, dense[:, cut : cut + experts], RATE_ROUTER, DECAY),
-            (vectors, vectors_first, vectors_second, dense[:, cut + experts : used].T, RATE_VECTORS, 0.0),
-            (hidden_bias, hidden_first, hidden_second, hidden_grad, RATE_HIDDEN, 0.0),
-            (return_bias, return_first, return_second, return_grad, RATE_RETURN, 0.0),
-        ],
-    )
+        [inner_grad[0], outer_grad[0], hidden_grad, return_grad],
+    )
+    inner_new, outer_new, projection_new, output_new, router_new, vectors_new, hidden_new, return_new = states
     return (
         block_output[None],
         input_grad[None],
-        jnp.sqrt(jnp.sum(squares)),
+        grad_norm,
         *projection_new,
         *output_new,
-        *router_new,
+        *(v.T for v in router_new),
         *vectors_new,
         *(v[None] for v in inner_new),
         *hidden_new,

time: 314 us -> 291 us (0.927)
  local copies, waits for them, and re-layouts: 19 us -> 6.49 us
  Pallas kernels: 284 us -> 277 us
    unnamed x53 -> x7, local copies, waits for them, and re-layouts: 14.8 us -> 3.69 us
    pallas_call x3 -> x2, Pallas kernels: 113 us -> 105 us  [the longest x1 76 us: backward(): pl.pallas_call(functools.partial(backward_kernel, dp, experts, capacity,...]
where the time goes in v1:
time: 291 us; the launch traced here: 288 us
  Pallas kernels  277 us (95%)
  local copies, waits for them, and re-layouts  6.49 us (2%)
  other arithmetic  3.23 us (1%)
    pallas_call x1, Pallas kernels, mixture(): pl.pallas_call(functools.partial(moe_kernel, dp, experts, chunk), out_sha...  109 us
    pallas_call x1, Pallas kernels, backward(): pl.pallas_call(functools.partial(backward_kernel, dp, experts, capacity,...  76 us
    pallas_call x1, Pallas kernels, gather_blocks(): pl.pallas_call(functools.partial(gather_kernel, dp, experts), out_shape=j...  33.7 us
    pallas_call x1, Pallas kernels, forward(): pl.pallas_call(functools.partial(forward_kernel, experts, capacity, chunk...  29.3 us
    pallas_call x1, Pallas kernels, adam_all(): pl.pallas_call(functools.partial(adam_kernel, experts), grid=(steps,), ou...  29 us

profile of v1, /device:TPU:0, one launch (start us, length us, event | category | flops | bytes accessed | tf_op | source)
XLA Modules:
  0.0 288.1 jit_solution(1379638074776503364)
XLA Ops:
  0.7 0.7 convert.21
  1.4 0.1 copy.66
  1.5 0.7 convert.20
  2.2 0.1 copy.67
  2.2 0.9 convert.19
  3.1 0.9 convert.18
  4.1 0.1 reshape.80
  4.2 0.1 copy.65
  4.3 0.1 reshape.81
  4.4 0.8 concatenate.4.in_ref
  5.2 1.6 copy.64
  6.7 1.6 copy.68.rank_col
  8.3 33.7 %gather_dense.1 = bf16[32,24,3200]{2,1,0:T(8,128)(2,1)} custom-call(bf16[24,3200]{1,0:T(8,128)(2,1)} %concatenate.4.in_ref), custom_call_target="tpu_custom_call" | custom-call | tf_op jit(solution)/shard_map/gather_dense/pallas_call | solution.py:563
  42.0 29.3 %attend_forward.1 = (bf16[128,3456]{1,0:T(8,128)(2,1)}, bf16[128,3456]{1,0:T(8,128)(2,1)}, bf16[576,2304]{1,0:T(8,128)(2,1)}, bf16[576,768]{1,0:T(8,128)(2,1)}, ...) custom-call(bf16[576,768]{1,0:T(8,128)(2,1)} %bitcast.60, ...), custom_call_target="tpu_custom_call" | custom-call | flops 6000000000 | bytes 20000000 | tf_op jit(solution)/shard_map/attend_forward/pallas_call | solution.py:763
  71.3 109.4 %mixture.1 = (bf16[16,8,3456]{2,1,0:T(8,128)(2,1)}, bf16[16,8,3456]{2,1,0:T(8,128)(2,1)}, bf16[1,768,1536]{2,1,0:T(8,128)(2,1)}, f32[1,1536]{1,0:T(1,128)}, bf16...) custom-call(bf16[16,8,3456]{2,1,0:T(8,128)(2,1)} %bitcast.69, bf16[16,8,3456]{2,1,0:T(8,128)(2,1)} %bitcast.70, ...), custom_call_target="tpu_custom_call" | custom-call | flops 16999999488 | bytes 25000000 | tf_op jit(solution)/shard_map/mixture/pallas_call | solution.py:1615
  180.8 76.0 %attend_backward.1 = (bf16[576,768]{1,0:T(8,128)(2,1)}, f32[576,768]{1,0:T(8,128)}, f32[24,3328]{1,0:T(8,128)}, f32[8,128]{1,0:T(8,128)}) custom-call(bf16[576,768]{1,0:T(8,128)(2,1)} %bitcast.61, bf16[576,768]{1,0:T(8,128)(2,1)} %bitcast.63, s32[576,2]{1,0:T(8,128)} %bitcast.48, bf16[128,3456]{1,0:T(8,128)(2,1)} %bitcast.67, ...), custom_call_target="tpu_custom_call" | custom-call | flops 15000000512 | bytes 30000000 | tf_op jit(solution)/shard_map/attend_backward/pallas_call | solution.py:1240
  256.7 0.0 copy-start.1
  256.7 0.0 copy-start
  256.8 29.0 %adam_all.1 = (f32[768,1536]{1,0:T(8,128)}, f32[768,1536]{1,0:T(8,128)}, f32[768,1536]{1,0:T(8,128)}, f32[1536,768]{1,0:T(8,128)}, f32[1536,768]{1,0:T(8,128)}, ...) custom-call(f32[8,128]{1,0:T(8,128)} %get-tuple-element.86.norm_ref,, ...), custom_call_target="tpu_custom_call" | custom-call | flops 50000000 | bytes 62000000 | tf_op jit(solution)/shard_map/adam_all/pallas_call | solution.py:1729
  285.7 0.0 copy-done.1
  285.7 0.9 copy.71
  286.6 0.0 copy-done
  286.6 1.2 copy.72
  (1 shorter events, 0.0 us)
Async XLA Ops:
  256.7 29.0 %copy-start.1 = (bf16[576,768]{1,0:T(8,128)(2,1)S(1)}, bf16[576,768]{1,0:T(8,128)(2,1)}, u32[]{:S(2)}) copy-start(bf16[576,768]{1,0:T(8,128)(2,1)} %get-tuple-element.84) | copy-start | bytes 2654212
  256.7 29.9 %copy-start = (f32[576,768]{1,0:T(8,128)S(1)}, f32[576,768]{1,0:T(8,128)}, u32[]{:S(2)}) copy-start(f32[576,768]{1,0:T(8,128)} %get-tuple-element.85) | copy-start | bytes 5308420
